TPU v7x, 256 devices: a whole 4x4x8 slice. The times are simulated.
256 devices in a mesh: comp: 128 (over x, z, y), tile: 2 (over core).
Axes of the slice: x: 4, y: 4, z: 8, core: 2. Of those that a mesh axis runs over, the one named last changes fastest.
Arguments:
- adjoint_final: float32 [1152, 128, 256], P('comp', None, 'tile'), may hold values from -6 to 6
- background: float32 [2, 1152, 128, 256], P(None, None, 'comp', 'tile'), as said below
- friction_velocity: float32 [2, 128, 256], P(None, 'comp', 'tile'), may hold values from 0.3 to 1.5
- wind_direction: float32 [2, 128, 256], P(None, 'comp', 'tile'), may hold values from -3.140625 to 3.140625
- refraction_rate: float32 [32, 128, 256], P(None, 'comp', 'tile'), may hold values from -0.45 to 0.45
- courant: float32 [32], replicated, may hold values from 0.2 to 0.63
- growth_rate: float32 [32], replicated, may hold values from 0.05 to 0.25
- dissipation_rate: float32 [32], replicated, may hold values from 0.05 to 0.3
- sea_mask: int32 [128, 256], replicated, may hold values 0 or 1
- interp_index: int32 [4, 128, 256], P(None, 'comp', 'tile'), may hold values from 0 to 2047, as said below
- interp_weight: float32 [4, 128, 256], P(None, 'comp', 'tile'), may hold values from 0 to 1, as said below
Outputs:
- adjoint_initial: float32 [1152, 128, 256], P('comp', None, 'tile')
- stress_gradient: float32 [2048, 2], P(('comp', 'tile'))
Inputs may be any that keep to these rules, and one draw needn't show every extreme that they name: `interp_index`: the four forcing cells around the grid cell; forcing cells carry numbers that are a permutation of the forcing grid's cells, the same for all grid cells. `interp_weight`: the four weights of a cell are positive and sum to one. `background`: positive spectra.
All inputs are finite; a program needn't handle non-finite values.
Results may differ from a plain program's by a relative error of at most 0.0001.
Values sent between devices are 32-bit elements; how exact they have to be, the bound alone decides.
No kernel may reach another device: no remote copies, remote signals or barrier semaphores. Data moves between devices by JAX's collectives and lax.ppermute only.
A program may use at most 64 MiB of HBM per device.

v0:
```python
import math

import jax
import jax.numpy as jnp
from jax import lax
from jax.sharding import PartitionSpec as P

NDIR = 36
NFREQ = 32
NSTEP = 2
COARSEN = 4


def extended(value, sides, width):
    for axis, dim in sides:
        peers, length = (lax.axis_size(axis), value.shape[dim])
        up = [(i, (i + 1) % peers) for i in range(peers - 1)]
        down = [(j, i) for i, j in up]
        last = lax.slice_in_dim(value, length - width, length, axis=dim)
        initial = lax.slice_in_dim(value, 0, width, axis=dim)
        before = lax.ppermute(last, axis, up)
        after = lax.ppermute(initial, axis, down)
        value = jnp.concatenate([before, value, after], axis=dim)
    return value


def spectral_angles():
    return jnp.arange(NDIR, dtype=jnp.int32).astype(jnp.float32) * (2.0 * math.pi / NDIR)


def flux_rates(first, count, courant):
    component = first + jnp.arange(count, dtype=jnp.int32)
    freq_index = component // NDIR
    dir_index = component % NDIR
    speed = jnp.sum(
        jnp.where(
            freq_index[:, None] == jnp.arange(NFREQ, dtype=jnp.int32)[None, :],
            courant[None, :],
            0.0,
        ),
        axis=1,
    )
    theta = dir_index.astype(jnp.float32) * (2.0 * math.pi / NDIR)
    return (speed * jnp.cos(theta), speed * jnp.sin(theta))


def stencil_adjoint(padded, padded_mask, east_rate, north_rate):
    centre_mask = padded_mask[1:-1, 1:-1]
    face_next_row = centre_mask * padded_mask[2:, 1:-1]
    face_prev_row = centre_mask * padded_mask[:-2, 1:-1]
    face_next_col = centre_mask * padded_mask[1:-1, 2:]
    face_prev_col = centre_mask * padded_mask[1:-1, :-2]
    east_pos = jnp.maximum(east_rate, 0.0)[:, None, None]
    east_neg = jnp.minimum(east_rate, 0.0)[:, None, None]
    north_pos = jnp.maximum(north_rate, 0.0)[:, None, None]
    north_neg = jnp.minimum(north_rate, 0.0)[:, None, None]
    centre = padded[:, 1:-1, 1:-1]
    diagonal = (
        1.0
        - east_pos * face_next_row
        + east_neg * face_prev_row
        - north_pos * face_next_col
        + north_neg * face_prev_col
    )
    result = centre * diagonal
    result = result - east_neg * face_prev_row * padded[:, :-2, 1:-1]
    result = result + east_pos * face_next_row * padded[:, 2:, 1:-1]
    result = result - north_neg * face_prev_col * padded[:, 1:-1, :-2]
    result = result + north_pos * face_next_col * padded[:, 1:-1, 2:]
    return result


def source_adjoint(
    adjoint, spectrum, friction, wind, sea_cells, growth_rate, dissipation_rate, refraction_rate
):
    theta = spectral_angles()
    spread = jnp.maximum(jnp.cos(theta[:, None, None] - wind[None]), 0.0)
    energy = jnp.sum(spectrum, axis=(0, 1)) / NFREQ
    growth = growth_rate[:, None, None, None]
    dissip = dissipation_rate[:, None, None, None]
    damped = jnp.sum(dissip * spectrum * adjoint, axis=(0, 1))
    stress = sea_cells * jnp.sum(growth * spread[None] * spectrum * adjoint, axis=(0, 1))
    diagonal = (
        1.0 + growth * friction[None, None] * spread[None] - dissip * (energy * energy)[None, None]
    )
    updated = sea_cells * (adjoint * diagonal - 2.0 / NFREQ * energy * damped)
    turn_pos = jnp.maximum(refraction_rate, 0.0)[:, None]
    turn_neg = jnp.minimum(refraction_rate, 0.0)[:, None]
    keep = (1.0 - jnp.abs(refraction_rate))[:, None]
    turned = (
        keep * updated
        - turn_neg * jnp.roll(updated, 1, axis=1)
        + turn_pos * jnp.roll(updated, -1, axis=1)
    )
    return (turned, stress)


def forcing_terms(weighted, corner_cells, count):
    inside = (corner_cells >= 0) & (corner_cells < count)
    target = jnp.where(inside, corner_cells, count)
    return jax.ops.segment_sum(weighted, target, num_segments=count + 1)[:count]


def shards(
    adjoint_final,
    background,
    friction_velocity,
    wind_direction,
    refraction_rate,
    courant,
    growth_rate,
    dissipation_rate,
    sea_mask,
    interp_index,
    interp_weight,
):
    comp_count = lax.axis_size("comp")
    tile_count = lax.axis_size("tile")
    comp_index = lax.axis_index("comp")
    tile_index = lax.axis_index("tile")
    local_comps, grid_rows, col_count = adjoint_final.shape
    row_count = grid_rows // comp_count
    all_comps = local_comps * comp_count
    grid_cols = col_count * tile_count
    owned_cells = grid_rows // COARSEN * (grid_cols // COARSEN) // (comp_count * tile_count)
    sea_cells = sea_mask.astype(jnp.float32)
    padded_mask = jnp.pad(sea_cells, 1)
    col_start = tile_index * col_count
    strip_mask = lax.dynamic_slice(
        padded_mask, (jnp.int32(0), col_start), (grid_rows + 2, col_count + 2)
    )
    block_mask = lax.dynamic_slice(
        padded_mask, (comp_index * row_count, col_start), (row_count + 2, col_count + 2)
    )
    point_mask = block_mask[1:-1, 1:-1]
    corner_cells = interp_index.reshape(-1)
    weighted_steps = [None] * NSTEP
    reduced_steps = [None] * NSTEP

    def local_sources(adjoint_points, step):
        spectrum = background[step].reshape(NFREQ, NDIR, row_count, col_count)
        turned, stress = source_adjoint(
            adjoint_points.reshape(NFREQ, NDIR, row_count, col_count),
            spectrum,
            friction_velocity[step],
            wind_direction[step],
            point_mask,
            growth_rate,
            dissipation_rate,
            refraction_rate,
        )
        weighted = (interp_weight * stress[None]).reshape(-1)
        weighted_steps[step] = weighted
        reduced_steps[step] = lax.psum_scatter(
            forcing_terms(weighted, corner_cells, owned_cells * lax.axis_size(("comp", "tile"))),
            ("comp", "tile"),
            scatter_dimension=0,
            tiled=True,
        )
        return turned.reshape(all_comps, row_count, col_count)

    adjoint = adjoint_final
    east_rate, north_rate = flux_rates(comp_index * local_comps, local_comps, courant)
    strip_centre = strip_mask[1:-1, 1:-1]
    for step in reversed(range(NSTEP)):
        adjoint_points = lax.all_to_all(adjoint, "comp", split_axis=1, concat_axis=0, tiled=True)
        adjoint_points = local_sources(adjoint_points, step)
        adjoint = lax.all_to_all(adjoint_points, "comp", split_axis=0, concat_axis=1, tiled=True)
        rimmed = extended(adjoint * strip_centre[None], (("tile", 2),), 1)
        padded = jnp.pad(rimmed, ((0, 0), (1, 1), (0, 0)))
        adjoint = stencil_adjoint(padded, strip_mask, east_rate, north_rate)
    gradient = jnp.stack(reduced_steps, axis=1)
    return (adjoint, gradient)


def solution(mesh):
    in_specs = (
        P("comp", None, "tile"),
        P(None, None, "comp", "tile"),
        P(None, "comp", "tile"),
        P(None, "comp", "tile"),
        P(None, "comp", "tile"),
        P(),
        P(),
        P(),
        P(),
        P(None, "comp", "tile"),
        P(None, "comp", "tile"),
    )
    out_specs = (P("comp", None, "tile"), P(("comp", "tile"), None))
    return jax.shard_map(shards, mesh=mesh, in_specs=in_specs, out_specs=out_specs, check_vma=False)
```

profile of v0, /device:TPU:1, one launch (start us, length us, event | category | flops | bytes accessed | tf_op | source)
XLA Modules:
  0.0 243.5 jit_solution(14121174326176869341)
XLA Ops:
  0.6 2.4 %copy.98 = f32[9,128,128]{2,0,1:T(8,128)} copy(f32[9,128,128]{2,1,0:T(8,128)} %param.11) | data formatting | bytes 1179648 | tf_op args[0]
  3.1 16.5 %all-to-all-start = ((f32[9,128,128]{2,0,1:T(8,128)}), f32[9,128,128]{2,0,1:T(8,128)S(1)}, u32[]{:S(2)}, u32[]{:S(2)}) async-start(f32[9,128,128]{2,0,1:T(8,128)} %copy.98), calls=%async_computation | async-start | bytes 2097152 | tf_op jit(solution)/shard_map/all_to_all | solution.py:166
  23.6 3.0 %slice_reduce_fusion = (f32[128]{0:T(128)S(1)}, f32[128]{0:T(128)S(1)}, f32[1,1152,1,128]{3,2,1,0:T(1,128)}, f32[1,1152,1,128]{3,2,1,0:T(1,128)S(1)}) fusion(f32[2,1152,1,128]{3,2,1,0:T(1,128)} %param.12), kind=kLoop, calls=%fused_computation.119 | loop fusion | flops 294656 | bytes 2360320 | tf_op jit(solution)/shard_map/reduce_sum | solution.py:78
  26.7 20.2 %all-to-all-done = f32[9,128,128]{2,0,1:T(8,128)S(1)} async-done(((f32[9,128,128]{2,0,1:T(8,128)}), f32[9,128,128]{2,0,1:T(8,128)S(1)}, u32[]{:S(2)}, u32[]{:S(2)}) %all-to-all-start) | async-done | bytes 589856 | tf_op jit(solution)/shard_map/all_to_all | solution.py:166
  46.9 1.6 fusion.17
  51.4 1.6 fusion.39
  54.0 1.7 pad_maximum_fusion.4
  57.3 9.1 %all-to-all-start.1 = ((f32[1152,1,128]{2,1,0:T(1,128)}), f32[1152,1,128]{2,1,0:T(1,128)S(1)}, u32[]{:S(2)}, u32[]{:S(2)}) async-start(f32[1152,1,128]{2,1,0:T(1,128)} %bitcast.17), calls=%async_computation.1 | async-start | bytes 1179648 | tf_op jit(solution)/shard_map/all_to_all | solution.py:168
  68.8 15.1 %all-to-all-done.1 = f32[1152,1,128]{2,1,0:T(1,128)S(1)} async-done(((f32[1152,1,128]{2,1,0:T(1,128)}), f32[1152,1,128]{2,1,0:T(1,128)S(1)}, u32[]{:S(2)}, u32[]{:S(2)}) %all-to-all-start.1) | async-done | bytes 589856 | tf_op jit(solution)/shard_map/all_to_all | solution.py:168
  84.9 1.3 collective-permute-start
  86.4 6.6 %collective-permute-start.1 = (f32[9,128,1]{1,2,0:T(1,128)S(1)}, f32[9,128,1]{1,2,0:T(1,128)}, u32[]{:S(2)}, u32[]{:S(2)}) collective-permute-start(f32[9,128,1]{1,2,0:T(1,128)S(1)} %copy.109), channel_id=1, source_target_pairs={{1,0},{3,2},{5,4},{7,6},{9,8},{11,10},{13,12},{15,14},{17,16},{19,... | collective-permute-start | bytes 13832 | tf_op jit(solution)/shard_map/ppermute | solution.py:22
  93.0 1.3 broadcast_maximum_fusion.2
  97.4 1.3 copy.114
  98.8 7.0 %all-to-all-start.2 = ((f32[9,128,128]{2,0,1:T(8,128)}), f32[9,128,128]{2,0,1:T(8,128)S(1)}, u32[]{:S(2)}, u32[]{:S(2)}) async-start(f32[9,128,128]{2,0,1:T(8,128)} %copy.114), calls=%async_computation.2 | async-start | bytes 2097152 | tf_op jit(solution)/shard_map/all_to_all | solution.py:166
  107.9 27.9 %all-to-all-done.2 = f32[9,128,128]{2,0,1:T(8,128)S(1)} async-done(((f32[9,128,128]{2,0,1:T(8,128)}), f32[9,128,128]{2,0,1:T(8,128)S(1)}, u32[]{:S(2)}, u32[]{:S(2)}) %all-to-all-start.2) | async-done | bytes 589856 | tf_op jit(solution)/shard_map/all_to_all | solution.py:166
  135.8 1.8 fusion.20
  140.9 1.1 multiply_add_fusion.2
  142.0 7.3 %all-to-all-start.3 = ((f32[1152,1,128]{2,1,0:T(1,128)}), f32[1152,1,128]{2,1,0:T(1,128)S(1)}, u32[]{:S(2)}, u32[]{:S(2)}) async-start(f32[1152,1,128]{2,1,0:T(1,128)} %bitcast.34), calls=%async_computation.3 | async-start | bytes 1179648 | tf_op jit(solution)/shard_map/all_to_all | solution.py:168
  149.4 3.8 %scatter_custom_fusion = f32[2049]{0:T(1024)S(1)} fusion(s32[512]{0:T(512)S(1)} %bitcast.110, f32[512]{0:T(512)S(1)} %bitcast.109, f32[]{:T(128)} %constant.19.clone.1), kind=kCustom, calls=%fused_computation.87 | custom fusion | flops 512 | bytes 8200 | tf_op jit(solution)/shard_map/scatter-add | solution.py:101
  153.3 3.6 %scatter_custom_fusion.1 = f32[2049]{0:T(1024)S(1)} fusion(s32[512]{0:T(512)S(1)} %bitcast.111, f32[512]{0:T(512)S(1)} %bitcast.108, f32[]{:T(128)} %constant.19.clone.1), kind=kCustom, calls=%fused_computation.85 | custom fusion | flops 512 | bytes 8200 | tf_op jit(solution)/shard_map/scatter-add | solution.py:101
  156.9 77.6 %all-reduce.5 = (f32[2048]{0:T(1024)S(1)}, f32[2048]{0:T(1024)S(1)}) all-reduce(f32[2048]{0:T(1024)S(1)} %slice.178, f32[2048]{0:T(1024)S(1)} %slice.177), channel_id=3, replica_groups=mesh['comp'=128,'tile'=2] {'comp','tile'}, use_global_device_ids=true, to_apply=%region_10.11.clone | all-reduce | flops 4096 | bytes 32768
  235.1 1.3 collective-permute-start.2
  236.6 3.0 %collective-permute-start.3 = (f32[9,128,1]{1,2,0:T(1,128)S(1)}, f32[9,128,1]{1,2,0:T(1,128)S(1)}, u32[]{:S(2)}, u32[]{:S(2)}) collective-permute-start(f32[9,128,1]{1,2,0:T(1,128)S(1)} %copy.125), channel_id=1, source_target_pairs={{1,0},{3,2},{5,4},{7,6},{9,8},{11,10},{13,12},{15,14},{17,16},{19,... | collective-permute-start | bytes 13832 | tf_op jit(solution)/shard_map/ppermute | solution.py:22
  241.7 1.8 fusion.6
  (156 shorter events, 24.1 us)
Async XLA Ops:
  3.1 16.5 %copy-start.39 = (f32[2,1,128]{2,1,0:T(1,128)S(1)}, f32[2,1,128]{2,1,0:T(1,128)}, u32[]{:S(2)}) copy-start(f32[2,1,128]{2,1,0:T(1,128)} %param.14) | copy-start | bytes 3076
  3.1 43.8 %all-to-all-start = ((f32[9,128,128]{2,0,1:T(8,128)}), f32[9,128,128]{2,0,1:T(8,128)S(1)}, u32[]{:S(2)}, u32[]{:S(2)}) async-start(f32[9,128,128]{2,0,1:T(8,128)} %copy.98), calls=%async_computation | async-start | bytes 2097152 | tf_op jit(solution)/shard_map/all_to_all | solution.py:166
  21.7 25.1 %copy-start.28 = (f32[128]{0:T(128)}, f32[128]{0:T(128)S(1)}, u32[]{:S(2)}) copy-start(f32[128]{0:T(128)S(1)} %mul.827) | copy-start | bytes 1540
  21.9 24.9 %copy-start.30 = (f32[128]{0:T(128)}, f32[128]{0:T(128)S(1)}, u32[]{:S(2)}) copy-start(f32[128]{0:T(128)S(1)} %mul.905) | copy-start | bytes 1540
  26.7 22.5 %copy-start.37 = (f32[128]{0:T(128)}, f32[128]{0:T(128)S(1)}, u32[]{:S(2)}) copy-start(f32[128]{0:T(128)S(1)} %get-tuple-element.10) | copy-start | bytes 1540
  50.4 5.8 %copy-start.18 = (f32[1,128]{1,0:T(1,128)}, f32[1,128]{1,0:T(1,128)S(1)}, u32[]{:S(2)}) copy-start(f32[1,128]{1,0:T(1,128)S(1)} %get-tuple-element.15) | copy-start | bytes 1540
  56.2 10.3 %copy-start.41 = (f32[32]{0:T(128)S(1)}, f32[32]{0:T(128)}, u32[]{:S(2)}) copy-start(f32[32]{0:T(128)} %param.16) | copy-start | bytes 388
  57.3 26.6 %all-to-all-start.1 = ((f32[1152,1,128]{2,1,0:T(1,128)}), f32[1152,1,128]{2,1,0:T(1,128)S(1)}, u32[]{:S(2)}, u32[]{:S(2)}) async-start(f32[1152,1,128]{2,1,0:T(1,128)} %bitcast.17), calls=%async_computation.1 | async-start | bytes 1179648 | tf_op jit(solution)/shard_map/all_to_all | solution.py:168
  68.0 15.9 %copy-start.4 = (f32[128,128]{1,0:T(8,128)}, f32[128,128]{1,0:T(8,128)S(1)}, u32[]{:S(2)}) copy-start(f32[128,128]{1,0:T(8,128)S(1)} %get-tuple-element.18) | copy-start | bytes 196612
  84.9 9.4 %collective-permute-start = (f32[9,128,1]{1,2,0:T(1,128)}, f32[9,128,1]{1,2,0:T(1,128)S(1)}, u32[]{:S(2)}, u32[]{:S(2)}) collective-permute-start(f32[9,128,1]{1,2,0:T(1,128)} %copy.108), channel_id=1, source_target_pairs={{0,1},{2,3},{4,5},{6,7},{8,9},{10,11},{12,13},{14,15},{16,17},{18,... | collective-permute-start | bytes 13832 | tf_op jit(solution)/shard_map/ppermute | solution.py:21
  86.4 8.1 %collective-permute-start.1 = (f32[9,128,1]{1,2,0:T(1,128)S(1)}, f32[9,128,1]{1,2,0:T(1,128)}, u32[]{:S(2)}, u32[]{:S(2)}) collective-permute-start(f32[9,128,1]{1,2,0:T(1,128)S(1)} %copy.109), channel_id=1, source_target_pairs={{1,0},{3,2},{5,4},{7,6},{9,8},{11,10},{13,12},{15,14},{17,16},{19,... | collective-permute-start | bytes 13832 | tf_op jit(solution)/shard_map/ppermute | solution.py:22
  98.8 7.0 %copy-start.14 = (f32[36,128]{1,0:T(8,128)S(1)}, f32[36,128]{1,0:T(8,128)}, u32[]{:S(2)}) copy-start(f32[36,128]{1,0:T(8,128)} %get-tuple-element.57) | copy-start | bytes 55300
  98.8 37.0 %all-to-all-start.2 = ((f32[9,128,128]{2,0,1:T(8,128)}), f32[9,128,128]{2,0,1:T(8,128)S(1)}, u32[]{:S(2)}, u32[]{:S(2)}) async-start(f32[9,128,128]{2,0,1:T(8,128)} %copy.114), calls=%async_computation.2 | async-start | bytes 2097152 | tf_op jit(solution)/shard_map/all_to_all | solution.py:166
  106.9 28.8 %copy-start.29 = (f32[128]{0:T(128)S(1)}, f32[128]{0:T(128)}, u32[]{:S(2)}) copy-start(f32[128]{0:T(128)} %copy-done.28) | copy-start | bytes 1540
  106.9 28.8 %copy-start.31 = (f32[128]{0:T(128)S(1)}, f32[128]{0:T(128)}, u32[]{:S(2)}) copy-start(f32[128]{0:T(128)} %copy-done.30) | copy-start | bytes 1540
  135.8 2.4 copy-start.38
  135.8 2.4 copy-start.19
  140.9 8.5 %copy-start.36 = (s32[4,1,128]{2,1,0:T(1,128)S(1)}, s32[4,1,128]{2,1,0:T(1,128)}, u32[]{:S(2)}) copy-start(s32[4,1,128]{2,1,0:T(1,128)} %param.20) | copy-start | bytes 6148
  140.9 8.5 %copy-start.32 = (f32[128]{0:T(128)S(1)}, f32[128]{0:T(128)}, u32[]{:S(2)}) copy-start(f32[128]{0:T(128)} %get-tuple-element.14) | copy-start | bytes 1540
  140.9 8.5 %copy-start.35 = (f32[4,1,128]{2,1,0:T(1,128)S(1)}, f32[4,1,128]{2,1,0:T(1,128)}, u32[]{:S(2)}) copy-start(f32[4,1,128]{2,1,0:T(1,128)} %param.21) | copy-start | bytes 6148
  142.0 92.6 %copy-start.5 = (f32[128,128]{1,0:T(8,128)S(1)}, f32[128,128]{1,0:T(8,128)}, u32[]{:S(2)}) copy-start(f32[128,128]{1,0:T(8,128)} %copy-done.4) | copy-start | bytes 196612
  142.0 92.6 %all-to-all-start.3 = ((f32[1152,1,128]{2,1,0:T(1,128)}), f32[1152,1,128]{2,1,0:T(1,128)S(1)}, u32[]{:S(2)}, u32[]{:S(2)}) async-start(f32[1152,1,128]{2,1,0:T(1,128)} %bitcast.34), calls=%async_computation.3 | async-start | bytes 1179648 | tf_op jit(solution)/shard_map/all_to_all | solution.py:168
  235.1 5.1 %collective-permute-start.2 = (f32[9,128,1]{1,2,0:T(1,128)S(1)}, f32[9,128,1]{1,2,0:T(1,128)S(1)}, u32[]{:S(2)}, u32[]{:S(2)}) collective-permute-start(f32[9,128,1]{1,2,0:T(1,128)S(1)} %copy.124), channel_id=1, source_target_pairs={{0,1},{2,3},{4,5},{6,7},{8,9},{10,11},{12,13},{14,15},{16,17},{18,... | collective-permute-start | bytes 13832 | tf_op jit(solution)/shard_map/ppermute | solution.py:21
  236.6 3.9 %collective-permute-start.3 = (f32[9,128,1]{1,2,0:T(1,128)S(1)}, f32[9,128,1]{1,2,0:T(1,128)S(1)}, u32[]{:S(2)}, u32[]{:S(2)}) collective-permute-start(f32[9,128,1]{1,2,0:T(1,128)S(1)} %copy.125), channel_id=1, source_target_pairs={{1,0},{3,2},{5,4},{7,6},{9,8},{11,10},{13,12},{15,14},{17,16},{19,... | collective-permute-start | bytes 13832 | tf_op jit(solution)/shard_map/ppermute | solution.py:22
  (26 other events, 31.0 us)
where the time goes:
time: 245 us; the launch traced here: 243 us
  blocking collectives  77.6 us (32%)
  waiting for transfers between devices  63.1 us (26%)
  starting transfers between devices  52.1 us (21%)
  other arithmetic  32.3 us (13%)
  local copies, waits for them, and re-layouts  16.9 us (7%)
    unnamed x1, blocking collectives  77.6 us
    all_to_all x2, waiting for transfers between devices, shards(): lax.all_to_all(adjoint, 'comp', split_axis=1, concat_axis=0, tiled=True)  48.1 us
    all_to_all x2, starting transfers between devices, shards(): lax.all_to_all(adjoint, 'comp', split_axis=1, concat_axis=0, tiled=True)  23.5 us
    all_to_all x2, starting transfers between devices, shards(): lax.all_to_all(adjoint_points, 'comp', split_axis=0, concat_axis=1, tiled...  16.5 us
    all_to_all x2, waiting for transfers between devices, shards(): lax.all_to_all(adjoint_points, 'comp', split_axis=0, concat_axis=1, tiled...  15.1 us
    ppermute x2, starting transfers between devices, extended(): after = lax.ppermute(initial, axis, down)  9.63 us
    scatter-add x2, other arithmetic, forcing_terms(): return jax.ops.segment_sum(weighted, target, num_segments=count + 1)[:count]  7.41 us
  transfers between devices with their start and end apart: 8, of which 3 were waited for; matrix products, arithmetic and copies ran while one was open for 9% of the time, Pallas kernels for 0%

commit v1 on v0

v1 whole, which is shorter than its diff:
```python
import math

import jax
import jax.numpy as jnp
import numpy as np
from jax import lax
from jax.experimental import pallas as pl
from jax.experimental.pallas import tpu as pltpu
from jax.sharding import PartitionSpec as P

NDIR = 36
NFREQ = 32
NSTEP = 2
NCOMP = NDIR * NFREQ
NX = 128
LANES = 128
LOCAL = 9
QUART = 4
SENT = LOCAL + 1
CELLS = 16

THETA = np.arange(NDIR) * (2.0 * math.pi / NDIR)
COS = np.cos(THETA)
SIN = np.sin(THETA)
EAST = list(range(28, NDIR)) + list(range(0, 10))
WEST = list(range(10, 28))
assert all(COS[d] > 0 for d in EAST) and all(COS[d] < 0 for d in WEST)
ORDER = EAST + WEST
PLACE = {d: p for p, d in enumerate(ORDER)}
HALF = len(EAST) * NFREQ

GROWTH, DISSIP, KEEP, TURN_NEG, TURN_POS, UP, DOWN, RIGHT, LEFT, GAIN0, GAIN1, LOSS0, LOSS1 = range(13)
GAIN, LOSS = (GAIN0, GAIN1), (LOSS0, LOSS1)

PARAMS = pltpu.CompilerParams(vmem_limit_bytes=24 * 1024 * 1024)


def lane_iota(rows):
    return lax.broadcasted_iota(jnp.int32, (rows, LANES), 1)


def sub_iota(rows):
    return lax.broadcasted_iota(jnp.int32, (rows, LANES), 0)


def by_row_kernel(in_ref, out_ref):
    for j in range(LOCAL):
        out_ref[pl.ds(j, NX, stride=LOCAL), :] = in_ref[j]


def prepare_kernel(
    spectrum_ref, friction_ref, wind_ref, refraction_ref, courant_ref, growth_ref, dissip_ref, mask_ref,
    coef_ref, spread_ref, vec_ref, face_ref, rate_ref,
):
    row = lax.axis_index("comp")
    tile = lax.axis_index("tile")
    left_half = mask_ref[:, :LANES].astype(jnp.float32)
    right_half = mask_ref[:, LANES:].astype(jnp.float32)
    first = tile == 0
    own = jnp.where(first, left_half, right_half)
    lane = lane_iota(NX)
    sub = sub_iota(NX)
    other = jnp.where(first, right_half, left_half)
    nxt = jnp.where(lane == LANES - 1, jnp.where(first, pltpu.roll(other, LANES - 1, 1), 0.0), pltpu.roll(own, LANES - 1, 1))
    prv = jnp.where(lane == 0, jnp.where(first, 0.0, pltpu.roll(other, 1, 1)), pltpu.roll(own, 1, 1))
    face_ref[0] = own * jnp.where(sub == NX - 1, 0.0, pltpu.roll(own, NX - 1, 0))
    face_ref[1] = own * jnp.where(sub == 0, 0.0, pltpu.roll(own, 1, 0))
    face_ref[2] = own * nxt
    face_ref[3] = own * prv
    pick = sub == row
    mask = jnp.sum(jnp.where(pick, own, 0.0), axis=0, keepdims=True)
    faces = [face_ref[k, pl.ds(row, 1), :] for k in range(4)]

    sub_f = sub_iota(NFREQ)
    growth = jnp.zeros((NFREQ, LANES), jnp.float32)
    dissip = jnp.zeros((NFREQ, LANES), jnp.float32)
    courant = jnp.zeros((NFREQ, LANES), jnp.float32)
    for f in range(NFREQ):
        at = sub_f == f
        growth = jnp.where(at, growth_ref[f], growth)
        dissip = jnp.where(at, dissip_ref[f], dissip)
        courant = jnp.where(at, courant_ref[f], courant)
    turn = refraction_ref[...]
    coef_ref[GROWTH] = growth
    coef_ref[DISSIP] = dissip
    coef_ref[KEEP] = 1.0 - jnp.abs(turn)
    coef_ref[TURN_NEG] = jnp.minimum(turn, 0.0)
    coef_ref[TURN_POS] = jnp.maximum(turn, 0.0)
    for k, name in enumerate((UP, DOWN, RIGHT, LEFT)):
        coef_ref[name] = courant * faces[k]
    vec_ref[...] = jnp.zeros_like(vec_ref)
    vec_ref[2:3] = mask
    theta = sub_iota(NDIR).astype(jnp.float32) * (2.0 * math.pi / NDIR)
    for n in range(NSTEP):
        total = jnp.zeros((8, LANES), jnp.float32)
        for k in range(NCOMP // 8):
            total = total + spectrum_ref[n, pl.ds(8 * k, 8), :]
        energy = jnp.sum(total, axis=0, keepdims=True) / NFREQ
        vec_ref[n : n + 1] = (2.0 / NFREQ) * energy * mask
        coef_ref[GAIN[n]] = growth * (friction_ref[n : n + 1] * mask)
        coef_ref[LOSS[n]] = mask - dissip * (energy * energy * mask)
        spread_ref[n] = jnp.maximum(jnp.cos(theta - wind_ref[n : n + 1]), 0.0)

    number = (row % QUART) * LOCAL + sub_iota(16)
    angle = number.astype(jnp.float32) * (2.0 * math.pi / NDIR)
    speed = courant_ref[row // QUART]
    rate_ref[0] = speed * jnp.cos(angle)
    rate_ref[1] = speed * jnp.sin(angle)


def source_sums(adjoint_of, spectrum_ref, coef_ref, spread_ref, vec_ref, step):
    damped = jnp.zeros((8, LANES), jnp.float32)
    stress = jnp.zeros((8, LANES), jnp.float32)
    for b in range(NFREQ // 8):
        plain = jnp.zeros((8, LANES), jnp.float32)
        spread = jnp.zeros((8, LANES), jnp.float32)
        for p, d in enumerate(ORDER):
            product = spectrum_ref[step, pl.ds(8 * b * NDIR + d, 8, stride=NDIR), :] * adjoint_of(b, p, d)
            plain = plain + product
            spread = spread + spread_ref[step, d : d + 1, :] * product
        damped = damped + coef_ref[DISSIP, 8 * b : 8 * b + 8] * plain
        stress = stress + coef_ref[GROWTH, 8 * b : 8 * b + 8] * spread
    damped = jnp.sum(damped, axis=0, keepdims=True)
    stress = jnp.sum(stress, axis=0, keepdims=True)
    return vec_ref[step : step + 1] * damped, vec_ref[2:3] * stress


def source_update(adjoint_of, store, coef_ref, spread_ref, shared, step):
    shared = jnp.broadcast_to(shared, (8, LANES))
    for b in range(NFREQ // 8):
        rows = slice(8 * b, 8 * b + 8)
        gain, loss = coef_ref[GAIN[step], rows], coef_ref[LOSS[step], rows]
        keep, neg, pos = coef_ref[KEEP, rows], coef_ref[TURN_NEG, rows], coef_ref[TURN_POS, rows]

        def updated(d):
            return adjoint_of(b, PLACE[d], d) * (loss + gain * spread_ref[step, d : d + 1, :]) - shared

        before, here, first = updated(ORDER[-1]), updated(ORDER[0]), None
        first = here
        for p, d in enumerate(ORDER):
            after = updated(ORDER[p + 1]) if p + 1 < NDIR else first
            store(b, p, d, keep * here - neg * before + pos * after)
            before, here = here, after


def first_source_kernel(
    adjoint_ref, spectrum_ref, coef_ref, spread_ref, vec_ref, east_ref, west_ref, edge_ref, stress_ref
):
    step = NSTEP - 1

    def adjoint_of(b, p, d):
        return adjoint_ref[pl.ds(8 * b * NDIR + d, 8, stride=NDIR), :]

    shared, stress = source_sums(adjoint_of, spectrum_ref, coef_ref, spread_ref, vec_ref, step)
    stress_ref[...] = jnp.broadcast_to(stress, (8, LANES))
    lane = lane_iota(8)
    edges = [jnp.zeros((8, LANES), jnp.float32) for _ in range(NFREQ // 8)]

    def store(b, p, d, value):
        ref, at = (east_ref, p) if p < NDIR // 2 else (west_ref, p - NDIR // 2)
        ref[pl.ds(at * NFREQ + 8 * b, 8), :] = value
        column = value[:, :1] if SIN[d] >= 0 else value[:, LANES - 1 :]
        edges[b] = jnp.where(lane == p, column, edges[b])

    source_update(adjoint_of, store, coef_ref, spread_ref, shared, step)
    for b in range(NFREQ // 8):
        edge_ref[8 * b : 8 * b + 8] = edges[b]


def second_source_kernel(
    east_ref, west_ref, east_next_ref, west_prev_ref, edge_ref, spectrum_ref, coef_ref, spread_ref, vec_ref, stress_ref,
    index_ref, weight_ref, out_ref, held_ref,
):
    step = 0
    lane = lane_iota(8)

    def propagated(b, p, d):
        rows = slice(8 * b, 8 * b + 8)
        ref, near, face, at = (
            (east_ref, east_next_ref, UP, p) if p < NDIR // 2 else (west_ref, west_prev_ref, DOWN, p - NDIR // 2)
        )
        centre = ref[pl.ds(at * NFREQ + 8 * b, 8), :]
        row = near[pl.ds(at * NFREQ + 8 * b, 8), :]
        arrived = edge_ref[rows, p : p + 1]
        if SIN[d] >= 0:
            side, column = RIGHT, jnp.where(lane == LANES - 1, arrived, pltpu.roll(centre, LANES - 1, 1))
        else:
            side, column = LEFT, jnp.where(lane == 0, arrived, pltpu.roll(centre, 1, 1))
        value = (
            centre
            + abs(float(COS[d])) * (coef_ref[face, rows] * (row - centre))
            + abs(float(SIN[d])) * (coef_ref[side, rows] * (column - centre))
        )
        held_ref[pl.ds(p * NFREQ + 8 * b, 8), :] = value
        return value

    shared, stress = source_sums(propagated, spectrum_ref, coef_ref, spread_ref, vec_ref, step)

    cells = jnp.zeros((NX, LANES), jnp.float32)
    sub = sub_iota(NX)
    for corner in range(4):
        index = index_ref[corner : corner + 1, :]
        owner = jnp.where(sub == index // CELLS, 1.0, 0.0)
        cell = index % CELLS
        weight = weight_ref[corner : corner + 1, :]
        values = jnp.where(sub == cell, weight * stress, 0.0)
        values = values + jnp.where(sub == cell + CELLS, weight * stress_ref[:1], 0.0)
        cells = cells + lax.dot_general(
            owner,
            values,
            (((1,), (1,)), ((), ())),
            precision=lax.Precision.HIGHEST,
            preferred_element_type=jnp.float32,
        )
    out_ref[pl.ds(LOCAL, NX, stride=SENT), :] = cells

    def adjoint_of(b, p, d):
        return held_ref[pl.ds(p * NFREQ + 8 * b, 8), :]

    def store(b, p, d, value):
        at = 8 * b * QUART * SENT + d // LOCAL * SENT + d % LOCAL
        out_ref[pl.ds(at, 8, stride=QUART * SENT), :] = value

    source_update(adjoint_of, store, coef_ref, spread_ref, shared, step)


def edges_kernel(arrived_ref, out_ref):
    lane = lane_iota(NX)
    edges = jnp.zeros((NX, LANES), jnp.float32)
    for j in range(LOCAL):
        value = arrived_ref[pl.ds(j, NX, stride=SENT), :]
        edges = jnp.where(lane == j, value[:, :1], edges)
        edges = jnp.where(lane == 16 + j, value[:, LANES - 1 :], edges)
    out_ref[:NX] = edges
    cells = arrived_ref[pl.ds(LOCAL, NX, stride=SENT), :]
    out_ref[NX:] = jnp.broadcast_to(jnp.sum(cells, axis=0, keepdims=True), (8, LANES))


def last_kernel(arrived_ref, mine_ref, edges_ref, face_ref, rate_ref, adjoint_ref, gradient_ref):
    tile = lax.axis_index("tile")
    lane = lane_iota(NX)
    for j in range(LOCAL):
        centre = arrived_ref[pl.ds(j, NX, stride=SENT), :]
        east, north = rate_ref[0, j : j + 1], rate_ref[1, j : j + 1]
        up = pltpu.roll(centre, NX - 1, 0) - centre
        down = pltpu.roll(centre, 1, 0) - centre
        right = jnp.where(lane == LANES - 1, edges_ref[:NX, j : j + 1], pltpu.roll(centre, LANES - 1, 1)) - centre
        left = jnp.where(lane == 0, edges_ref[:NX, 16 + j : 17 + j], pltpu.roll(centre, 1, 1)) - centre
        value = centre + jnp.maximum(east, 0.0) * (face_ref[0] * up) - jnp.minimum(east, 0.0) * (face_ref[1] * down)
        value = value + jnp.maximum(north, 0.0) * (face_ref[2] * right) - jnp.minimum(north, 0.0) * (face_ref[3] * left)
        adjoint_ref[j] = value
    cells = mine_ref[NX : NX + 1] + edges_ref[NX : NX + 1]
    at = lane_iota(8) - sub_iota(8) - tile * (CELLS // 2)
    for n in range(NSTEP):
        gradient_ref[:, n : n + 1] = jnp.sum(jnp.where(at == n * CELLS, cells, 0.0), axis=1, keepdims=True)


def f32(*shape):
    return jax.ShapeDtypeStruct(shape, jnp.float32)


def spec(*spaces):
    return [pl.BlockSpec(memory_space=pltpu.SMEM if s == "s" else pltpu.VMEM) for s in spaces[0]]


def call(kernel, inputs, out_shape, scratch=()):
    single = not isinstance(out_shape, tuple)
    return pl.pallas_call(
        kernel,
        in_specs=spec(inputs),
        out_specs=spec("v")[0] if single else tuple(spec("v" * len(out_shape))),
        out_shape=out_shape,
        scratch_shapes=list(scratch),
        compiler_params=PARAMS,
    )


def shards(
    adjoint_final,
    background,
    friction_velocity,
    wind_direction,
    refraction_rate,
    courant,
    growth_rate,
    dissipation_rate,
    sea_mask,
    interp_index,
    interp_weight,
):
    comp_count = lax.axis_size("comp")
    spectrum = background.reshape(NSTEP, NCOMP, LANES)
    by_row = call(by_row_kernel, "v", f32(NCOMP, LANES))(adjoint_final)
    points = lax.all_to_all(by_row.reshape(NCOMP, 1, LANES), "comp", split_axis=0, concat_axis=0, tiled=True)
    points = points.reshape(NCOMP, LANES)
    coef, spread, vec, face, rate = call(
        prepare_kernel,
        "vvvvsssv",
        (f32(13, NFREQ, LANES), f32(NSTEP, NDIR, LANES), f32(8, LANES), f32(4, NX, LANES), f32(2, 16, LANES)),
    )(
        spectrum,
        friction_velocity.reshape(NSTEP, LANES),
        wind_direction.reshape(NSTEP, LANES),
        refraction_rate.reshape(NFREQ, LANES),
        courant,
        growth_rate,
        dissipation_rate,
        sea_mask,
    )
    east, west, edge, stress = call(
        first_source_kernel, "vvvvv", (f32(HALF, LANES), f32(HALF, LANES), f32(NFREQ, LANES), f32(8, LANES))
    )(points, spectrum, coef, spread, vec)
    swap = [(0, 1), (1, 0)]
    east_next = lax.ppermute(east, "comp", [(i + 1, i) for i in range(comp_count - 1)])
    west_prev = lax.ppermute(west, "comp", [(i, i + 1) for i in range(comp_count - 1)])
    edge = lax.ppermute(edge, "tile", swap)
    sent = call(
        second_source_kernel,
        "vvvvvvvvvvvv",
        f32(NX * SENT, LANES),
        [pltpu.VMEM((NCOMP, LANES), jnp.float32)],
    )(
        east, west, east_next, west_prev, edge, spectrum, coef, spread, vec, stress,
        interp_index.reshape(4, LANES), interp_weight.reshape(4, LANES),
    )
    arrived = lax.all_to_all(sent.reshape(NX * SENT, 1, LANES), "comp", split_axis=0, concat_axis=0, tiled=True)
    arrived = arrived.reshape(NX * SENT, LANES)
    mine = call(edges_kernel, "v", f32(NX + 8, LANES))(arrived)
    theirs = lax.ppermute(mine, "tile", swap)
    return call(last_kernel, "vvvvv", (f32(LOCAL, NX, LANES), f32(8, NSTEP)))(arrived, mine, theirs, face, rate)


def solution(mesh):
    in_specs = (
        P("comp", None, "tile"),
        P(None, None, "comp", "tile"),
        P(None, "comp", "tile"),
        P(None, "comp", "tile"),
        P(None, "comp", "tile"),
        P(),
        P(),
        P(),
        P(),
        P(None, "comp", "tile"),
        P(None, "comp", "tile"),
    )
    out_specs = (P("comp", None, "tile"), P(("comp", "tile"), None))
    return jax.shard_map(shards, mesh=mesh, in_specs=in_specs, out_specs=out_specs, check_vma=False)
```

time: 245 us -> 90 us (0.37)
  blocking collectives: 77.6 us -> 31.8 us
  waiting for transfers between devices: 63.1 us -> 18.6 us
  other arithmetic: 32.3 us -> 0 us
  starting transfers between devices: 52.1 us -> 31.3 us
  local copies, waits for them, and re-layouts: 16.9 us -> 1.83 us
  Pallas kernels: 0 us -> 5.45 us
    unnamed x1 -> x0, blocking collectives: 77.6 us -> none
    all_to_all x4 -> x1, waiting for transfers between devices: 63.1 us -> 16.9 us  [shards(): lax.all_to_all(by_row.reshape(NCOMP, 1, LANES), 'comp', split_axis=0, con...]
    all_to_all x0 -> x1, blocking collectives: none -> 31.8 us  [shards(): lax.all_to_all(sent.reshape(NX * SENT, 1, LANES), 'comp', split_axis=0, c...]
    all_to_all x4 -> x1, starting transfers between devices: 39.9 us -> 16.3 us  [shards(): lax.all_to_all(by_row.reshape(NCOMP, 1, LANES), 'comp', split_axis=0, con...]
    scatter-add x2 -> x0, other arithmetic: 7.41 us -> none  [forcing_terms(): return jax.ops.segment_sum(weighted, target, num_segments=count + 1)[:count]]
    reduce_sum x4 -> x0, other arithmetic: 7.18 us -> none  [the longest x2 3.4 us: source_adjoint(): jnp.sum(growth * spread[None] * spectrum * adjoint, axis=(0, 1))]
    pallas_call x0 -> x6, Pallas kernels: none -> 5.45 us  [the longest x1 1.58 us: shards(): call(last_kernel, 'vvvvv', (f32(LOCAL, NX, LANES), f32(8, NSTEP)))]
    mul x14 -> x0, other arithmetic: 4.99 us -> none  [the longest x3 1.96 us: source_adjoint(): updated = sea_cells * (adjoint * diagonal - 2.0 / NFREQ * energy * damped)]
  transfers between devices with their start and end apart: 8 -> 5, of which waited for: 3 -> 3; matrix products, arithmetic and copies ran while one was open for 9% -> 0% of each run, Pallas kernels for 0% -> 1%
where the time goes in v1:
time: 90 us; the launch traced here: 89.8 us
  blocking collectives  31.8 us (35%)
  starting transfers between devices  31.3 us (35%)
  waiting for transfers between devices  18.6 us (21%)
  Pallas kernels  5.45 us (6%)
  local copies, waits for them, and re-layouts  1.83 us (2%)
    all_to_all x1, blocking collectives, shards(): lax.all_to_all(sent.reshape(NX * SENT, 1, LANES), 'comp', split_axis=0, c...  31.8 us
    all_to_all x1, waiting for transfers between devices, shards(): lax.all_to_all(by_row.reshape(NCOMP, 1, LANES), 'comp', split_axis=0, con...  16.9 us
    all_to_all x1, starting transfers between devices, shards(): lax.all_to_all(by_row.reshape(NCOMP, 1, LANES), 'comp', split_axis=0, con...  16.3 us
    ppermute x1, starting transfers between devices, shards(): theirs = lax.ppermute(mine, 'tile', swap)  5.46 us
    ppermute x1, starting transfers between devices, shards(): edge = lax.ppermute(edge, 'tile', swap)  4.21 us
    ppermute x1, starting transfers between devices, shards(): lax.ppermute(west, 'comp', [(i, i + 1) for i in range(comp_count - 1)])  4 us
  transfers between devices with their start and end apart: 5, of which 3 were waited for; matrix products, arithmetic and copies ran while one was open for 0% of the time, Pallas kernels for 1%

profile of v1, /device:TPU:1, one launch (start us, length us, event | category | flops | bytes accessed | tf_op | source)
XLA Modules:
  0.0 89.8 jit_solution(1030683553944336266)
XLA Ops:
  0.6 0.0 copy-start
  0.6 0.0 copy-start.1
  0.7 1.1 %copy-done.1 = f32[9,128,128]{2,1,0:T(8,128)S(1)} copy-done((f32[9,128,128]{2,1,0:T(8,128)S(1)}, f32[9,128,128]{2,1,0:T(8,128)}, u32[]{:S(2)}) %copy-start.1) | copy-done | bytes 589848
  1.8 0.9 shard_map.122
  2.7 16.3 %all-to-all-start = ((f32[1152,1,128]{2,1,0:T(1,128)}), f32[1152,1,128]{2,1,0:T(1,128)S(1)}, u32[]{:S(2)}, u32[]{:S(2)}) async-start(f32[1152,1,128]{2,1,0:T(1,128)} %bitcast.1), calls=%async_computation | async-start | bytes 1179648 | tf_op jit(solution)/shard_map/all_to_all | solution.py:294
  19.1 1.0 %shard_map.123 = (f32[13,32,128]{2,1,0:T(8,128)S(1)}, f32[2,36,128]{2,1,0:T(8,128)S(1)}, f32[8,128]{1,0:T(8,128)S(1)}, f32[4,128,128]{2,1,0:T(8,128)S(1)}, f32[2,16,128]{2,1,0:T(8,128)S(1)}) custom-call(f32[2,1152,128]{2,1,0:T(8,128)S(1)} %bitcast.14, f32[2,128]{1,0:T(2,128)S(1)} %bitcast.24, f32[2,128]{1,0:T(2,128)S(1)} %bitcast.25, ...), custom_call_target="tpu_custom_call" | custom-call | tf_op jit(solution)/shard_map/pallas_call | solution.py:296
  20.1 0.0 copy-start.4
  20.1 0.0 copy-start.5
  20.1 16.9 %all-to-all-done = f32[1152,1,128]{2,1,0:T(1,128)S(1)} async-done(((f32[1152,1,128]{2,1,0:T(1,128)}), f32[1152,1,128]{2,1,0:T(1,128)S(1)}, u32[]{:S(2)}, u32[]{:S(2)}) %all-to-all-start) | async-done | bytes 589856 | tf_op jit(solution)/shard_map/all_to_all | solution.py:294
  37.0 0.4 shard_map.124
  37.3 1.3 %collective-permute-start = (f32[576,128]{1,0:T(8,128)S(1)}, f32[576,128]{1,0:T(8,128)S(1)}, u32[]{:S(2)}, u32[]{:S(2)}) collective-permute-start(f32[576,128]{1,0:T(8,128)S(1)} %get-tuple-element.14.east_ref), channel_id=1, source_target_pairs={{2,0},{4,2},{6,4},{8,6},{10,8},{12,10},{14,12},{16,14},{18,16},{20... | collective-permute-start | bytes 884744 | tf_op jit(solution)/shard_map/ppermute | solution.py:314
  38.6 4.0 %collective-permute-start.1 = (f32[576,128]{1,0:T(8,128)S(1)}, f32[576,128]{1,0:T(8,128)S(1)}, u32[]{:S(2)}, u32[]{:S(2)}) collective-permute-start(f32[576,128]{1,0:T(8,128)S(1)} %get-tuple-element.15.west_ref), channel_id=1, source_target_pairs={{0,2},{2,4},{4,6},{6,8},{8,10},{10,12},{12,14},{14,16},{16,18},{18... | collective-permute-start | bytes 884744 | tf_op jit(solution)/shard_map/ppermute | solution.py:315
  42.7 4.2 %collective-permute-start.2 = (f32[32,128]{1,0:T(8,128)S(1)}, f32[32,128]{1,0:T(8,128)S(1)}, u32[]{:S(2)}, u32[]{:S(2)}) collective-permute-start(f32[32,128]{1,0:T(8,128)S(1)} %get-tuple-element.16), channel_id=1, source_target_pairs={{0,1},{1,0},{2,3},{3,2},{4,5},{5,4},{6,7},{7,6},{8,9},{9,8},{10,11... | collective-permute-start | bytes 49160 | tf_op jit(solution)/shard_map/ppermute | solution.py:316
  46.9 0.8 collective-permute-done.2.edge_ref
  47.7 0.0 collective-permute-done.east_next_ref
  47.7 0.0 collective-permute-done.1.west_prev_ref
  47.7 0.0 copy-done.4
  47.7 1.3 %shard_map.125 = f32[1280,128]{1,0:T(8,128)S(1)} custom-call(f32[576,128]{1,0:T(8,128)S(1)} %get-tuple-element.14.east_ref, f32[576,128]{1,0:T(8,128)S(1)} %get-tuple-element.15.west_ref, f32[576,128]{1,0:T(8,128)S(1)} %collective-permute-done.east_next_ref, f32[576,128]{1,0:T(8,128)S(1)} %collective-permute-done.1.west_prev_ref, ...), custom_call_target="tpu_custom_call" | custom-call | tf_op jit(solution)/shard_map/pallas_call | solution.py:317
  49.0 31.8 %all_to_all.10 = f32[1280,1,128]{2,1,0:T(1,128)S(1)} all-to-all(f32[1280,1,128]{2,1,0:T(1,128)S(1)} %bitcast.19), channel_id=1, replica_groups=mesh['comp'=128,'tile'=2] {'comp'}, dimensions={0} | all-to-all | bytes 1310720 | tf_op jit(solution)/shard_map/all_to_all | solution.py:326
  80.8 0.4 shard_map.126.mine_ref
  81.2 5.5 %collective-permute-start.3 = (f32[136,128]{1,0:T(8,128)S(1)}, f32[136,128]{1,0:T(8,128)S(1)}, u32[]{:S(2)}, u32[]{:S(2)}) collective-permute-start(f32[136,128]{1,0:T(8,128)S(1)} %shard_map.126.mine_ref), channel_id=1, source_target_pairs={{0,1},{1,0},{2,3},{3,2},{4,5},{5,4},{6,7},{7,6},{8,9},{9,8},{10,11... | collective-permute-start | bytes 208904 | tf_op jit(solution)/shard_map/ppermute | solution.py:329
  86.6 0.9 %collective-permute-done.3.edges_ref = f32[136,128]{1,0:T(8,128)S(1)} collective-permute-done((f32[136,128]{1,0:T(8,128)S(1)}, f32[136,128]{1,0:T(8,128)S(1)}, u32[]{:S(2)}, u32[]{:S(2)}) %collective-permute-start.3) | collective-permute-done | bytes 69664 | tf_op jit(solution)/shard_map/ppermute | solution.py:329
  87.6 1.6 %shard_map.127 = (f32[9,128,128]{2,1,0:T(8,128)}, f32[8,2]{1,0:T(8,128)S(1)}) custom-call(f32[1280,128]{1,0:T(8,128)S(1)} %bitcast.18, f32[136,128]{1,0:T(8,128)S(1)} %shard_map.126.mine_ref, f32[136,128]{1,0:T(8,128)S(1)} %collective-permute-done.3.edges_ref, f32[4,128,128]{2,1,0:T(8,128)S(1)} %get-tuple-element.18.face_ref, ...), custom_call_target="tpu_custom_call" | custom-call | tf_op jit(solution)/shard_map/pallas_call | solution.py:330
  89.1 0.6 copy.16
  (16 shorter events, 0.0 us)
Async XLA Ops:
  0.6 18.4 %copy-start = (f32[2,1152,1,128]{3,2,1,0:T(1,128)S(1)}, f32[2,1152,1,128]{3,2,1,0:T(1,128)}, u32[]{:S(2)}) copy-start(f32[2,1152,1,128]{3,2,1,0:T(1,128)} %param.12) | copy-start | bytes 3538948
  0.6 1.2 %copy-start.1 = (f32[9,128,128]{2,1,0:T(8,128)S(1)}, f32[9,128,128]{2,1,0:T(8,128)}, u32[]{:S(2)}) copy-start(f32[9,128,128]{2,1,0:T(8,128)} %in_ref.1) | copy-start | bytes 1769476
  1.8 17.3 %copy-start.2 = (s32[128,256]{1,0:T(8,128)S(1)}, s32[128,256]{1,0:T(8,128)}, u32[]{:S(2)}) copy-start(s32[128,256]{1,0:T(8,128)} %mask_ref.1) | copy-start | bytes 393220
  1.8 17.3 %copy-start.3 = (f32[32,1,128]{2,1,0:T(1,128)S(1)}, f32[32,1,128]{2,1,0:T(1,128)}, u32[]{:S(2)}) copy-start(f32[32,1,128]{2,1,0:T(1,128)} %param.15) | copy-start | bytes 49156
  1.8 17.3 %copy-start.6 = (f32[2,1,128]{2,1,0:T(1,128)S(1)}, f32[2,1,128]{2,1,0:T(1,128)}, u32[]{:S(2)}) copy-start(f32[2,1,128]{2,1,0:T(1,128)} %param.13) | copy-start | bytes 3076
  1.8 17.3 %copy-start.7 = (f32[2,1,128]{2,1,0:T(1,128)S(1)}, f32[2,1,128]{2,1,0:T(1,128)}, u32[]{:S(2)}) copy-start(f32[2,1,128]{2,1,0:T(1,128)} %param.14) | copy-start | bytes 3076
  1.8 17.3 %copy-start.8 = (f32[32]{0:T(128)S(1)}, f32[32]{0:T(128)}, u32[]{:S(2)}) copy-start(f32[32]{0:T(128)} %courant_ref.1) | copy-start | bytes 388
  1.8 17.3 %copy-start.9 = (f32[32]{0:T(128)S(1)}, f32[32]{0:T(128)}, u32[]{:S(2)}) copy-start(f32[32]{0:T(128)} %growth_ref.1) | copy-start | bytes 388
  1.8 17.3 %copy-start.10 = (f32[32]{0:T(128)S(1)}, f32[32]{0:T(128)}, u32[]{:S(2)}) copy-start(f32[32]{0:T(128)} %dissip_ref.1) | copy-start | bytes 388
  2.7 34.3 %all-to-all-start = ((f32[1152,1,128]{2,1,0:T(1,128)}), f32[1152,1,128]{2,1,0:T(1,128)S(1)}, u32[]{:S(2)}, u32[]{:S(2)}) async-start(f32[1152,1,128]{2,1,0:T(1,128)} %bitcast.1), calls=%async_computation | async-start | bytes 1179648 | tf_op jit(solution)/shard_map/all_to_all | solution.py:294
  20.1 27.6 %copy-start.4 = (s32[4,1,128]{2,1,0:T(1,128)S(1)}, s32[4,1,128]{2,1,0:T(1,128)}, u32[]{:S(2)}) copy-start(s32[4,1,128]{2,1,0:T(1,128)} %param.20) | copy-start | bytes 6148
  20.1 27.6 %copy-start.5 = (f32[4,1,128]{2,1,0:T(1,128)S(1)}, f32[4,1,128]{2,1,0:T(1,128)}, u32[]{:S(2)}) copy-start(f32[4,1,128]{2,1,0:T(1,128)} %param.21) | copy-start | bytes 6148
  37.3 10.4 %collective-permute-start = (f32[576,128]{1,0:T(8,128)S(1)}, f32[576,128]{1,0:T(8,128)S(1)}, u32[]{:S(2)}, u32[]{:S(2)}) collective-permute-start(f32[576,128]{1,0:T(8,128)S(1)} %get-tuple-element.14.east_ref), channel_id=1, source_target_pairs={{2,0},{4,2},{6,4},{8,6},{10,8},{12,10},{14,12},{16,14},{18,16},{20... | collective-permute-start | bytes 884744 | tf_op jit(solution)/shard_map/ppermute | solution.py:314
  38.6 9.1 %collective-permute-start.1 = (f32[576,128]{1,0:T(8,128)S(1)}, f32[576,128]{1,0:T(8,128)S(1)}, u32[]{:S(2)}, u32[]{:S(2)}) collective-permute-start(f32[576,128]{1,0:T(8,128)S(1)} %get-tuple-element.15.west_ref), channel_id=1, source_target_pairs={{0,2},{2,4},{4,6},{6,8},{8,10},{10,12},{12,14},{14,16},{16,18},{18... | collective-permute-start | bytes 884744 | tf_op jit(solution)/shard_map/ppermute | solution.py:315
  42.7 5.0 %collective-permute-start.2 = (f32[32,128]{1,0:T(8,128)S(1)}, f32[32,128]{1,0:T(8,128)S(1)}, u32[]{:S(2)}, u32[]{:S(2)}) collective-permute-start(f32[32,128]{1,0:T(8,128)S(1)} %get-tuple-element.16), channel_id=1, source_target_pairs={{0,1},{1,0},{2,3},{3,2},{4,5},{5,4},{6,7},{7,6},{8,9},{9,8},{10,11... | collective-permute-start | bytes 49160 | tf_op jit(solution)/shard_map/ppermute | solution.py:316
  81.2 6.4 %collective-permute-start.3 = (f32[136,128]{1,0:T(8,128)S(1)}, f32[136,128]{1,0:T(8,128)S(1)}, u32[]{:S(2)}, u32[]{:S(2)}) collective-permute-start(f32[136,128]{1,0:T(8,128)S(1)} %shard_map.126.mine_ref), channel_id=1, source_target_pairs={{0,1},{1,0},{2,3},{3,2},{4,5},{5,4},{6,7},{7,6},{8,9},{9,8},{10,11... | collective-permute-start | bytes 208904 | tf_op jit(solution)/shard_map/ppermute | solution.py:329

commit v2 on v1

v2 whole, which is shorter than its diff:
```python
import math

import jax
import jax.numpy as jnp
import numpy as np
from jax import lax
from jax.experimental import pallas as pl
from jax.experimental.pallas import tpu as pltpu
from jax.sharding import PartitionSpec as P

NDIR = 36
NFREQ = 32
NSTEP = 2
NCOMP = NDIR * NFREQ
NX = 128
LANES = 128
LOCAL = 9
QUART = 4
SENT = LOCAL + 1
CELLS = 16

THETA = np.arange(NDIR) * (2.0 * math.pi / NDIR)
COS = [0.0 if d % 18 == 9 else math.cos(t) for d, t in enumerate(THETA)]
SIN = [0.0 if d % 18 == 0 else math.sin(t) for d, t in enumerate(THETA)]
EAST = list(range(27, NDIR)) + list(range(0, 9))
WEST = list(range(9, 27))
assert all(COS[d] >= 0 for d in EAST) and all(COS[d] <= 0 for d in WEST)
assert all(SIN[d] >= 0 for d in range(18)) and all(SIN[d] <= 0 for d in range(18, 36))
ORDER = EAST + WEST
PLACE = {d: p for p, d in enumerate(ORDER)}
HALF = len(EAST) * NFREQ

GROWTH, DISSIP, KEEP, TURN_NEG, TURN_POS, UP, DOWN, RIGHT, LEFT, GAIN0, GAIN1, LOSS0, LOSS1 = range(13)
GAIN, LOSS = (GAIN0, GAIN1), (LOSS0, LOSS1)
PART = NSTEP * CELLS

PARAMS = pltpu.CompilerParams(vmem_limit_bytes=24 * 1024 * 1024)
WHOLE = pltpu.CompilerParams(vmem_limit_bytes=60 * 1024 * 1024)


def lane_iota(rows):
    return lax.broadcasted_iota(jnp.int32, (rows, LANES), 1)


def sub_iota(rows):
    return lax.broadcasted_iota(jnp.int32, (rows, LANES), 0)


def by_row_kernel(in_ref, out_ref, held_ref, sems):
    copies = [pltpu.make_async_copy(in_ref.at[j], held_ref.at[j], sems.at[j]) for j in range(LOCAL)]
    for copy in copies:
        copy.start()
    for j, copy in enumerate(copies):
        copy.wait()
        out_ref[pl.ds(j, NX, stride=LOCAL), :] = held_ref[j]


def prepare_kernel(
    spectrum_ref, friction_ref, wind_ref, refraction_ref, courant_ref, growth_ref, dissip_ref, mask_ref,
    index_ref, weight_ref, coef_ref, spread_ref, vec_ref, face_ref, owner_ref, cell_ref,
):
    row = lax.axis_index("comp")
    tile = lax.axis_index("tile")
    left_half = mask_ref[:, :LANES].astype(jnp.float32)
    right_half = mask_ref[:, LANES:].astype(jnp.float32)
    first = tile == 0
    own = jnp.where(first, left_half, right_half)
    lane = lane_iota(NX)
    sub = sub_iota(NX)
    other = jnp.where(first, right_half, left_half)
    nxt = jnp.where(lane == LANES - 1, jnp.where(first, pltpu.roll(other, LANES - 1, 1), 0.0), pltpu.roll(own, LANES - 1, 1))
    prv = jnp.where(lane == 0, jnp.where(first, 0.0, pltpu.roll(other, 1, 1)), pltpu.roll(own, 1, 1))
    quarter = row % QUART
    speed = courant_ref[row // QUART]
    up = own * jnp.where(sub == NX - 1, 0.0, pltpu.roll(own, NX - 1, 0))
    down = own * jnp.where(sub == 0, 0.0, pltpu.roll(own, 1, 0))
    right, left = own * nxt, own * prv
    face_ref[0] = speed * jnp.where((quarter == 0) | (quarter == 3), up, down)
    face_ref[1] = speed * jnp.where(quarter < 2, right, left)
    pick = sub == row
    mask, *faces = [
        jnp.sum(jnp.where(pick, value, 0.0), axis=0, keepdims=True) for value in (own, up, down, right, left)
    ]

    sub_f = sub_iota(NFREQ)
    growth = jnp.zeros((NFREQ, LANES), jnp.float32)
    dissip = jnp.zeros((NFREQ, LANES), jnp.float32)
    courant = jnp.zeros((NFREQ, LANES), jnp.float32)
    for f in range(NFREQ):
        at = sub_f == f
        growth = jnp.where(at, growth_ref[f], growth)
        dissip = jnp.where(at, dissip_ref[f], dissip)
        courant = jnp.where(at, courant_ref[f], courant)
    turn = refraction_ref[...]
    coef_ref[GROWTH] = growth
    coef_ref[DISSIP] = dissip
    coef_ref[KEEP] = 1.0 - jnp.abs(turn)
    coef_ref[TURN_NEG] = jnp.minimum(turn, 0.0)
    coef_ref[TURN_POS] = jnp.maximum(turn, 0.0)
    for k, name in enumerate((UP, DOWN, RIGHT, LEFT)):
        coef_ref[name] = courant * faces[k]
    vec_ref[...] = jnp.zeros_like(vec_ref)
    vec_ref[2:3] = mask
    theta = sub_iota(NDIR).astype(jnp.float32) * (2.0 * math.pi / NDIR)
    for n in range(NSTEP):
        total = jnp.zeros((8, LANES), jnp.float32)
        for k in range(NCOMP // 8):
            total = total + spectrum_ref[n, pl.ds(8 * k, 8), :]
        energy = jnp.sum(total, axis=0, keepdims=True) / NFREQ
        vec_ref[n : n + 1] = (2.0 / NFREQ) * energy * mask
        coef_ref[GAIN[n]] = growth * (friction_ref[n : n + 1] * mask)
        coef_ref[LOSS[n]] = mask - dissip * (energy * energy * mask)
        spread_ref[n] = jnp.maximum(jnp.cos(theta - wind_ref[n : n + 1]), 0.0)

    sub_c = sub_iota(PART)
    for corner in range(4):
        lanes = slice(corner * LANES, (corner + 1) * LANES)
        index = index_ref[corner : corner + 1, :]
        owner_ref[:, lanes] = jnp.where(sub == index // CELLS, 1.0, 0.0).astype(jnp.bfloat16)
        cell_ref[:, lanes] = jnp.where(sub_c % CELLS == index % CELLS, weight_ref[corner : corner + 1, :], 0.0)


def source_sums(adjoint_of, spectrum_ref, coef_ref, spread_ref, vec_ref, step):
    damped = jnp.zeros((8, LANES), jnp.float32)
    stress = jnp.zeros((8, LANES), jnp.float32)
    for b in range(NFREQ // 8):
        plain = jnp.zeros((8, LANES), jnp.float32)
        spread = jnp.zeros((8, LANES), jnp.float32)
        for p, d in enumerate(ORDER):
            product = spectrum_ref[step, pl.ds(8 * b * NDIR + d, 8, stride=NDIR), :] * adjoint_of(b, p, d)
            plain = plain + product
            spread = spread + spread_ref[step, d : d + 1, :] * product
        damped = damped + coef_ref[DISSIP, 8 * b : 8 * b + 8] * plain
        stress = stress + coef_ref[GROWTH, 8 * b : 8 * b + 8] * spread
    damped = jnp.sum(damped, axis=0, keepdims=True)
    stress = jnp.sum(stress, axis=0, keepdims=True)
    return vec_ref[step : step + 1] * damped, vec_ref[2:3] * stress


def source_update(adjoint_of, store, coef_ref, spread_ref, shared, step):
    shared = jnp.broadcast_to(shared, (8, LANES))
    for b in range(NFREQ // 8):
        rows = slice(8 * b, 8 * b + 8)
        gain, loss = coef_ref[GAIN[step], rows], coef_ref[LOSS[step], rows]
        keep, neg, pos = coef_ref[KEEP, rows], coef_ref[TURN_NEG, rows], coef_ref[TURN_POS, rows]

        def updated(d):
            return adjoint_of(b, PLACE[d], d) * (loss + gain * spread_ref[step, d : d + 1, :]) - shared

        before, here, first = updated(ORDER[-1]), updated(ORDER[0]), None
        first = here
        for p, d in enumerate(ORDER):
            after = updated(ORDER[p + 1]) if p + 1 < NDIR else first
            store(b, p, d, keep * here - neg * before + pos * after)
            before, here = here, after


def first_source_kernel(
    adjoint_ref, spectrum_ref, coef_ref, spread_ref, vec_ref, moved_ref, one_ref, two_ref, edge_ref, stress_ref
):
    step = NSTEP - 1

    def adjoint_of(b, p, d):
        return adjoint_ref[pl.ds(8 * b * NDIR + d, 8, stride=NDIR), :]

    shared, stress = source_sums(adjoint_of, spectrum_ref, coef_ref, spread_ref, vec_ref, step)
    stress_ref[...] = jnp.broadcast_to(stress, (8, LANES))
    lane = lane_iota(8)
    edges = [jnp.zeros((8, LANES), jnp.float32) for _ in range(NFREQ // 8)]

    def store(b, p, d, value):
        moved_ref[pl.ds(p * NFREQ + 8 * b, 8), :] = value
        column = value[:, :1] if SIN[d] >= 0 else value[:, LANES - 1 :]
        edges[b] = jnp.where(lane == p, column, edges[b])

    source_update(adjoint_of, store, coef_ref, spread_ref, shared, step)
    for b in range(NFREQ // 8):
        edge_ref[8 * b : 8 * b + 8] = edges[b]
    tile = lax.axis_index("tile")

    @pl.when(tile == 0)
    def _():
        one_ref[...] = moved_ref[:HALF]
        two_ref[...] = moved_ref[HALF:]

    @pl.when(tile == 1)
    def _():
        one_ref[...] = moved_ref[HALF:]
        two_ref[...] = moved_ref[:HALF]


def second_source_kernel(
    moved_ref, one_ref, two_ref, edge_ref, spectrum_ref, coef_ref, spread_ref, vec_ref, stress_ref,
    owner_ref, cell_ref, out_ref, held_ref,
):
    step = 0
    lane = lane_iota(8)
    first = jnp.broadcast_to(lax.axis_index("tile"), (8, LANES)) == 0

    def propagated(b, p, d):
        rows = slice(8 * b, 8 * b + 8)
        east = p < NDIR // 2
        face, at = (UP, p) if east else (DOWN, p - NDIR // 2)
        centre = moved_ref[pl.ds(p * NFREQ + 8 * b, 8), :]
        one = one_ref[pl.ds(at * NFREQ + 8 * b, 8), :]
        two = two_ref[pl.ds(at * NFREQ + 8 * b, 8), :]
        row = jnp.where(first, one, two) if east else jnp.where(first, two, one)
        arrived = edge_ref[rows, p : p + 1]
        if SIN[d] >= 0:
            side, column = RIGHT, jnp.where(lane == LANES - 1, arrived, pltpu.roll(centre, LANES - 1, 1))
        else:
            side, column = LEFT, jnp.where(lane == 0, arrived, pltpu.roll(centre, 1, 1))
        value = (
            centre
            + abs(COS[d]) * (coef_ref[face, rows] * (row - centre))
            + abs(SIN[d]) * (coef_ref[side, rows] * (column - centre))
        )
        held_ref[pl.ds(p * NFREQ + 8 * b, 8), :] = value
        return value

    shared, stress = source_sums(propagated, spectrum_ref, coef_ref, spread_ref, vec_ref, step)

    values = jnp.concatenate(
        [
            cell_ref[CELLS * n : CELLS * n + CELLS, :] * jnp.concatenate([row] * 4, axis=1)
            for n, row in enumerate((stress, stress_ref[:1]))
        ],
        axis=0,
    )
    parts = []
    for _ in range(3):
        parts.append(values.astype(jnp.bfloat16))
        values = values - parts[-1].astype(jnp.float32)
    parts.append(jnp.zeros_like(parts[0]))
    cells = lax.dot_general(
        owner_ref[...], jnp.concatenate(parts, axis=0), (((1,), (1,)), ((), ())), preferred_element_type=jnp.float32
    )
    out_ref[pl.ds(LOCAL, NX, stride=SENT), :] = cells

    def adjoint_of(b, p, d):
        return held_ref[pl.ds(p * NFREQ + 8 * b, 8), :]

    def store(b, p, d, value):
        at = 8 * b * QUART * SENT + d // LOCAL * SENT + d % LOCAL
        out_ref[pl.ds(at, 8, stride=QUART * SENT), :] = value

    source_update(adjoint_of, store, coef_ref, spread_ref, shared, step)


def edges_kernel(arrived_ref, out_ref):
    lane = lane_iota(NX)
    quarter = lax.axis_index("comp") % QUART
    for north in (True, False):

        @pl.when((quarter < 2) == north)
        def _():
            edges = jnp.zeros((NX, LANES), jnp.float32)
            for j in range(LOCAL):
                value = arrived_ref[pl.ds(j, NX, stride=SENT), :]
                edges = jnp.where(lane == j, value[:, :1] if north else value[:, LANES - 1 :], edges)
            out_ref[:NX] = edges

    cells = arrived_ref[pl.ds(LOCAL, NX, stride=SENT), :]
    out_ref[NX:] = jnp.broadcast_to(jnp.sum(cells, axis=0, keepdims=True), (8, LANES))


def last_kernel(arrived_ref, mine_ref, edges_ref, face_ref, adjoint_ref, gradient_ref, held_ref, sems):
    tile = lax.axis_index("tile")
    quarter = lax.axis_index("comp") % QUART
    lane = lane_iota(NX)
    copies = [pltpu.make_async_copy(held_ref.at[j], adjoint_ref.at[j], sems.at[j]) for j in range(LOCAL)]
    for q in range(QUART):

        @pl.when(quarter == q)
        def _():
            for j in range(LOCAL):
                d = q * LOCAL + j
                centre = arrived_ref[pl.ds(j, NX, stride=SENT), :]
                arrived = edges_ref[:NX, j : j + 1]
                row = pltpu.roll(centre, NX - 1 if d in EAST else 1, 0)
                if SIN[q * LOCAL + 1] > 0:
                    column = jnp.where(lane == LANES - 1, arrived, pltpu.roll(centre, LANES - 1, 1))
                else:
                    column = jnp.where(lane == 0, arrived, pltpu.roll(centre, 1, 1))
                held_ref[j] = (
                    centre
                    + abs(COS[d]) * (face_ref[0] * (row - centre))
                    + abs(SIN[d]) * (face_ref[1] * (column - centre))
                )
                copies[j].start()

    cells = mine_ref[NX:] + edges_ref[NX:]
    cells = cells + pltpu.roll(cells, LANES - PART, 1) + pltpu.roll(cells, LANES - 2 * PART, 1)
    for n in range(NSTEP):
        at = pltpu.roll(cells, LANES - n * CELLS - tile * (CELLS // 2), 1)
        gradient_ref[n : n + 1, :] = at[:1, : CELLS // 2]
    for copy in copies:
        copy.wait()


def f32(*shape):
    return jax.ShapeDtypeStruct(shape, jnp.float32)


SPACES = {"s": pltpu.SMEM, "v": pltpu.VMEM, "h": pltpu.HBM}


def spec(spaces):
    return [pl.BlockSpec(memory_space=SPACES[space]) for space in spaces]


def call(kernel, inputs, outputs, out_shape, scratch=(), params=PARAMS):
    single = len(outputs) == 1
    return pl.pallas_call(
        kernel,
        in_specs=spec(inputs),
        out_specs=spec(outputs)[0] if single else tuple(spec(outputs)),
        out_shape=out_shape,
        scratch_shapes=list(scratch),
        compiler_params=params,
    )


def shards(
    adjoint_final,
    background,
    friction_velocity,
    wind_direction,
    refraction_rate,
    courant,
    growth_rate,
    dissipation_rate,
    sea_mask,
    interp_index,
    interp_weight,
):
    comp_count = lax.axis_size("comp")
    spectrum = background.reshape(NSTEP, NCOMP, LANES)
    held = [pltpu.VMEM((LOCAL, NX, LANES), jnp.float32), pltpu.SemaphoreType.DMA((LOCAL,))]
    by_row = call(by_row_kernel, "h", "v", f32(NCOMP, LANES), held, WHOLE)(adjoint_final)
    points = lax.all_to_all(by_row.reshape(NCOMP, 1, LANES), "comp", split_axis=0, concat_axis=0, tiled=True)
    points = points.reshape(NCOMP, LANES)
    coef, spread, vec, face, owner, cell = call(
        prepare_kernel,
        "vvvvsssvvv",
        "vvvvvv",
        (
            f32(13, NFREQ, LANES),
            f32(NSTEP, NDIR, LANES),
            f32(8, LANES),
            f32(2, NX, LANES),
            jax.ShapeDtypeStruct((NX, 4 * LANES), jnp.bfloat16),
            f32(PART, 4 * LANES),
        ),
    )(
        spectrum,
        friction_velocity.reshape(NSTEP, LANES),
        wind_direction.reshape(NSTEP, LANES),
        refraction_rate.reshape(NFREQ, LANES),
        courant,
        growth_rate,
        dissipation_rate,
        sea_mask,
        interp_index.reshape(4, LANES),
        interp_weight.reshape(4, LANES),
    )
    moved, one, two, edge, stress = call(
        first_source_kernel,
        "vvvvv",
        "vvvvv",
        (f32(NCOMP, LANES), f32(HALF, LANES), f32(HALF, LANES), f32(NFREQ, LANES), f32(8, LANES)),
    )(points, spectrum, coef, spread, vec)
    swap = [(0, 1), (1, 0)]
    steps = range(comp_count - 1)
    turns = [
        [(2 * (i + 1) + t, 2 * i + t) for i in steps] + [(2 * i + 1 - t, 2 * (i + 1) + 1 - t) for i in steps]
        for t in range(2)
    ]
    one = lax.ppermute(one, ("comp", "tile"), turns[0])
    two = lax.ppermute(two, ("comp", "tile"), turns[1])
    edge = lax.ppermute(edge, "tile", swap)
    sent = call(
        second_source_kernel, "v" * 11, "v", f32(NX * SENT, LANES), [pltpu.VMEM((NCOMP, LANES), jnp.float32)]
    )(moved, one, two, edge, spectrum, coef, spread, vec, stress, owner, cell)
    arrived = lax.all_to_all(sent.reshape(NX * SENT, 1, LANES), "comp", split_axis=0, concat_axis=0, tiled=True)
    arrived = arrived.reshape(NX * SENT, LANES)
    mine = call(edges_kernel, "v", "v", f32(NX + 8, LANES))(arrived)
    theirs = lax.ppermute(mine, "tile", swap)
    adjoint, gradient = call(
        last_kernel, "vvvv", "hv", (f32(LOCAL, NX, LANES), f32(NSTEP, CELLS // 2)), held
    )(arrived, mine, theirs, face)
    return adjoint, gradient.T


def solution(mesh):
    in_specs = (
        P("comp", None, "tile"),
        P(None, None, "comp", "tile"),
        P(None, "comp", "tile"),
        P(None, "comp", "tile"),
        P(None, "comp", "tile"),
        P(),
        P(),
        P(),
        P(),
        P(None, "comp", "tile"),
        P(None, "comp", "tile"),
    )
    out_specs = (P("comp", None, "tile"), P(("comp", "tile"), None))
    return jax.shard_map(shards, mesh=mesh, in_specs=in_specs, out_specs=out_specs, check_vma=False)
```

time: 90 us -> 88.6 us (0.984)
  blocking collectives: 31.8 us -> 29.1 us
  waiting for transfers between devices: 18.6 us -> 21.1 us
  local copies, waits for them, and re-layouts: 1.83 us -> 0.04 us
    all_to_all x1, blocking collectives: 31.8 us -> 29.1 us  [shards(): lax.all_to_all(sent.reshape(NX * SENT, 1, LANES), 'comp', split_axis=0, c...]
    ppermute x2, waiting for transfers between devices: 0.01 us -> 2.5 us  [the longest x1 2.5 us: shards(): two = lax.ppermute(two, ('comp', 'tile'), turns[1])]
    unnamed x22 -> x20, local copies, waits for them, and re-layouts: 1.19 us -> 0.04 us
    ppermute x2, starting transfers between devices: 5.3 us -> 4.24 us  [the longest x1 2.95 us: shards(): one = lax.ppermute(one, ('comp', 'tile'), turns[0])]
    ppermute x1, starting transfers between devices: 4.21 us -> 5.24 us  [shards(): edge = lax.ppermute(edge, 'tile', swap)]
  transfers between devices with their start and end apart: 5 -> 5, of which waited for: 3 -> 4; matrix products, arithmetic and copies ran while one was open for 0% -> 0% of each run, Pallas kernels for 1% -> 1%
where the time goes in v2:
time: 88.6 us; the launch traced here: 88.3 us
  starting transfers between devices  31 us (35%)
  blocking collectives  29.1 us (33%)
  waiting for transfers between devices  21.1 us (24%)
  Pallas kernels  6.26 us (7%)
    all_to_all x1, blocking collectives, shards(): lax.all_to_all(sent.reshape(NX * SENT, 1, LANES), 'comp', split_axis=0, c...  29.1 us
    all_to_all x1, waiting for transfers between devices, shards(): lax.all_to_all(by_row.reshape(NCOMP, 1, LANES), 'comp', split_axis=0, con...  16.8 us
    all_to_all x1, starting transfers between devices, shards(): lax.all_to_all(by_row.reshape(NCOMP, 1, LANES), 'comp', split_axis=0, con...  16.3 us
    ppermute x1, starting transfers between devices, shards(): edge = lax.ppermute(edge, 'tile', swap)  5.24 us
    ppermute x1, starting transfers between devices, shards(): theirs = lax.ppermute(mine, 'tile', swap)  5.14 us
    ppermute x1, starting transfers between devices, shards(): one = lax.ppermute(one, ('comp', 'tile'), turns[0])  2.95 us
    ppermute x1, waiting for transfers between devices, shards(): two = lax.ppermute(two, ('comp', 'tile'), turns[1])  2.5 us
    pallas_call x1, Pallas kernels, shards(): call(by_row_kernel, 'h', 'v', f32(NCOMP, LANES), held, WHOLE)(adjoint_final)  2.09 us
  transfers between devices with their start and end apart: 5, of which 4 were waited for; matrix products, arithmetic and copies ran while one was open for 0% of the time, Pallas kernels for 1%

profile of v2, /device:TPU:1, one launch (start us, length us, event | category | flops | bytes accessed | tf_op | source)
XLA Modules:
  0.0 88.3 jit_solution(16593872967025467189)
XLA Ops:
  0.6 0.0 copy-start.4
  0.6 0.0 copy-start.3
  0.7 0.0 copy-start.1
  0.7 0.0 copy-start.9
  0.7 0.0 copy-start.8
  0.7 0.0 copy-start.7
  0.7 0.0 copy-start.2
  0.7 2.1 %shard_map.122 = f32[1152,128]{1,0:T(8,128)} custom-call(f32[9,128,128]{2,1,0:T(8,128)} %in_ref.1), custom_call_target="tpu_custom_call" | custom-call | tf_op jit(solution)/shard_map/pallas_call | solution.py:340
  2.8 16.3 %all-to-all-start = ((f32[1152,1,128]{2,1,0:T(1,128)}), f32[1152,1,128]{2,1,0:T(1,128)S(1)}, u32[]{:S(2)}, u32[]{:S(2)}) async-start(f32[1152,1,128]{2,1,0:T(1,128)} %bitcast.27), calls=%async_computation | async-start | bytes 1179648 | tf_op jit(solution)/shard_map/all_to_all | solution.py:341
  19.3 1.0 %shard_map.123 = (f32[13,32,128]{2,1,0:T(8,128)S(1)}, f32[2,36,128]{2,1,0:T(8,128)S(1)}, f32[8,128]{1,0:T(8,128)S(1)}, f32[2,128,128]{2,1,0:T(8,128)S(1)}, bf16[...) custom-call(f32[2,1152,128]{2,1,0:T(8,128)S(1)} %bitcast.15, f32[2,128]{1,0:T(2,128)S(1)} %bitcast.25, ...), custom_call_target="tpu_custom_call" | custom-call | tf_op jit(solution)/shard_map/pallas_call | solution.py:343
  20.3 16.8 %all-to-all-done = f32[1152,1,128]{2,1,0:T(1,128)S(1)} async-done(((f32[1152,1,128]{2,1,0:T(1,128)}), f32[1152,1,128]{2,1,0:T(1,128)S(1)}, u32[]{:S(2)}, u32[]{:S(2)}) %all-to-all-start) | async-done | bytes 589856 | tf_op jit(solution)/shard_map/all_to_all | solution.py:341
  37.1 0.4 shard_map.124
  37.5 2.9 %collective-permute-start = (f32[576,128]{1,0:T(8,128)S(1)}, f32[576,128]{1,0:T(8,128)S(1)}, u32[]{:S(2)}, u32[]{:S(2)}) collective-permute-start(f32[576,128]{1,0:T(8,128)S(1)} %get-tuple-element.19), channel_id=1, source_target_pairs={{2,0},{4,2},{6,4},{8,6},{10,8},{12,10},{14,12},{16,14},{18,16},{20... | collective-permute-start | bytes 884744 | tf_op jit(solution)/shard_map/ppermute | solution.py:379
  40.5 1.3 %collective-permute-start.1 = (f32[576,128]{1,0:T(8,128)S(1)}, f32[576,128]{1,0:T(8,128)S(1)}, u32[]{:S(2)}, u32[]{:S(2)}) collective-permute-start(f32[576,128]{1,0:T(8,128)S(1)} %get-tuple-element.20), channel_id=1, source_target_pairs={{3,1},{5,3},{7,5},{9,7},{11,9},{13,11},{15,13},{17,15},{19,17},{21... | collective-permute-start | bytes 884744 | tf_op jit(solution)/shard_map/ppermute | solution.py:380
  41.8 5.2 %collective-permute-start.2 = (f32[32,128]{1,0:T(8,128)S(1)}, f32[32,128]{1,0:T(8,128)S(1)}, u32[]{:S(2)}, u32[]{:S(2)}) collective-permute-start(f32[32,128]{1,0:T(8,128)S(1)} %get-tuple-element.21), channel_id=1, source_target_pairs={{0,1},{1,0},{2,3},{3,2},{4,5},{5,4},{6,7},{7,6},{8,9},{9,8},{10,11... | collective-permute-start | bytes 49160 | tf_op jit(solution)/shard_map/ppermute | solution.py:381
  47.0 0.8 collective-permute-done.2.edge_ref
  47.9 0.0 collective-permute-done.one_ref
  47.9 2.5 %collective-permute-done.1.two_ref = f32[576,128]{1,0:T(8,128)S(1)} collective-permute-done((f32[576,128]{1,0:T(8,128)S(1)}, f32[576,128]{1,0:T(8,128)S(1)}, u32[]{:S(2)}, u32[]{:S(2)}) %collective-permute-start.1) | collective-permute-done | bytes 294944 | tf_op jit(solution)/shard_map/ppermute | solution.py:380
  50.4 0.8 shard_map.125
  51.2 29.1 %all_to_all.10 = f32[1280,1,128]{2,1,0:T(1,128)S(1)} all-to-all(f32[1280,1,128]{2,1,0:T(1,128)S(1)} %bitcast.20), channel_id=1, replica_groups=mesh['comp'=128,'tile'=2] {'comp'}, dimensions={0} | all-to-all | bytes 1310720 | tf_op jit(solution)/shard_map/all_to_all | solution.py:385
  80.3 0.2 shard_map.126.mine_ref
  80.6 5.1 %collective-permute-start.3 = (f32[136,128]{1,0:T(8,128)S(1)}, f32[136,128]{1,0:T(8,128)S(1)}, u32[]{:S(2)}, u32[]{:S(2)}) collective-permute-start(f32[136,128]{1,0:T(8,128)S(1)} %shard_map.126.mine_ref), channel_id=1, source_target_pairs={{0,1},{1,0},{2,3},{3,2},{4,5},{5,4},{6,7},{7,6},{8,9},{9,8},{10,11... | collective-permute-start | bytes 208904 | tf_op jit(solution)/shard_map/ppermute | solution.py:388
  85.7 0.9 %collective-permute-done.3.edges_ref = f32[136,128]{1,0:T(8,128)S(1)} collective-permute-done((f32[136,128]{1,0:T(8,128)S(1)}, f32[136,128]{1,0:T(8,128)S(1)}, u32[]{:S(2)}, u32[]{:S(2)}) %collective-permute-start.3) | collective-permute-done | bytes 69664 | tf_op jit(solution)/shard_map/ppermute | solution.py:388
  86.6 1.7 %shard_map.127 = (f32[9,128,128]{2,1,0:T(8,128)}, f32[2,8]{1,0:T(2,128)}) custom-call(f32[1280,128]{1,0:T(8,128)S(1)} %bitcast.19, f32[136,128]{1,0:T(8,128)S(1)} %shard_map.126.mine_ref, f32[136,128]{1,0:T(8,128)S(1)} %collective-permute-done.3.edges_ref, f32[2,128,128]{2,1,0:T(8,128)S(1)} %get-tuple-element.25.face_ref), custom_call_target="tpu_custom_call" | custom-call | tf_op jit(solution)/shard_map/pallas_call | solution.py:389
  (13 shorter events, 0.0 us)
Async XLA Ops:
  0.6 18.6 %copy-start.4 = (f32[4,1,128]{2,1,0:T(1,128)S(1)}, f32[4,1,128]{2,1,0:T(1,128)}, u32[]{:S(2)}) copy-start(f32[4,1,128]{2,1,0:T(1,128)} %param.21) | copy-start | bytes 6148
  0.6 18.6 %copy-start.3 = (s32[4,1,128]{2,1,0:T(1,128)S(1)}, s32[4,1,128]{2,1,0:T(1,128)}, u32[]{:S(2)}) copy-start(s32[4,1,128]{2,1,0:T(1,128)} %param.20) | copy-start | bytes 6148
  0.7 18.6 %copy-start.1 = (s32[128,256]{1,0:T(8,128)S(1)}, s32[128,256]{1,0:T(8,128)}, u32[]{:S(2)}) copy-start(s32[128,256]{1,0:T(8,128)} %mask_ref.1) | copy-start | bytes 393220
  0.7 18.6 %copy-start.9 = (f32[32]{0:T(128)S(1)}, f32[32]{0:T(128)}, u32[]{:S(2)}) copy-start(f32[32]{0:T(128)} %dissip_ref.1) | copy-start | bytes 388
  0.7 18.6 %copy-start.8 = (f32[32]{0:T(128)S(1)}, f32[32]{0:T(128)}, u32[]{:S(2)}) copy-start(f32[32]{0:T(128)} %growth_ref.1) | copy-start | bytes 388
  0.7 18.6 %copy-start.7 = (f32[32]{0:T(128)S(1)}, f32[32]{0:T(128)}, u32[]{:S(2)}) copy-start(f32[32]{0:T(128)} %courant_ref.1) | copy-start | bytes 388
  0.7 18.6 %copy-start.2 = (f32[32,1,128]{2,1,0:T(1,128)S(1)}, f32[32,1,128]{2,1,0:T(1,128)}, u32[]{:S(2)}) copy-start(f32[32,1,128]{2,1,0:T(1,128)} %param.15) | copy-start | bytes 49156
  0.7 18.6 %copy-start.6 = (f32[2,1,128]{2,1,0:T(1,128)S(1)}, f32[2,1,128]{2,1,0:T(1,128)}, u32[]{:S(2)}) copy-start(f32[2,1,128]{2,1,0:T(1,128)} %param.14) | copy-start | bytes 3076
  0.7 18.6 %copy-start.5 = (f32[2,1,128]{2,1,0:T(1,128)S(1)}, f32[2,1,128]{2,1,0:T(1,128)}, u32[]{:S(2)}) copy-start(f32[2,1,128]{2,1,0:T(1,128)} %param.13) | copy-start | bytes 3076
  0.7 18.6 %copy-start = (f32[2,1152,1,128]{3,2,1,0:T(1,128)S(1)}, f32[2,1152,1,128]{3,2,1,0:T(1,128)}, u32[]{:S(2)}) copy-start(f32[2,1152,1,128]{3,2,1,0:T(1,128)} %param.12) | copy-start | bytes 3538948
  2.8 34.3 %all-to-all-start = ((f32[1152,1,128]{2,1,0:T(1,128)}), f32[1152,1,128]{2,1,0:T(1,128)S(1)}, u32[]{:S(2)}, u32[]{:S(2)}) async-start(f32[1152,1,128]{2,1,0:T(1,128)} %bitcast.27), calls=%async_computation | async-start | bytes 1179648 | tf_op jit(solution)/shard_map/all_to_all | solution.py:341
  37.5 10.3 %collective-permute-start = (f32[576,128]{1,0:T(8,128)S(1)}, f32[576,128]{1,0:T(8,128)S(1)}, u32[]{:S(2)}, u32[]{:S(2)}) collective-permute-start(f32[576,128]{1,0:T(8,128)S(1)} %get-tuple-element.19), channel_id=1, source_target_pairs={{2,0},{4,2},{6,4},{8,6},{10,8},{12,10},{14,12},{16,14},{18,16},{20... | collective-permute-start | bytes 884744 | tf_op jit(solution)/shard_map/ppermute | solution.py:379
  40.5 9.9 %collective-permute-start.1 = (f32[576,128]{1,0:T(8,128)S(1)}, f32[576,128]{1,0:T(8,128)S(1)}, u32[]{:S(2)}, u32[]{:S(2)}) collective-permute-start(f32[576,128]{1,0:T(8,128)S(1)} %get-tuple-element.20), channel_id=1, source_target_pairs={{3,1},{5,3},{7,5},{9,7},{11,9},{13,11},{15,13},{17,15},{19,17},{21... | collective-permute-start | bytes 884744 | tf_op jit(solution)/shard_map/ppermute | solution.py:380
  41.8 6.1 %collective-permute-start.2 = (f32[32,128]{1,0:T(8,128)S(1)}, f32[32,128]{1,0:T(8,128)S(1)}, u32[]{:S(2)}, u32[]{:S(2)}) collective-permute-start(f32[32,128]{1,0:T(8,128)S(1)} %get-tuple-element.21), channel_id=1, source_target_pairs={{0,1},{1,0},{2,3},{3,2},{4,5},{5,4},{6,7},{7,6},{8,9},{9,8},{10,11... | collective-permute-start | bytes 49160 | tf_op jit(solution)/shard_map/ppermute | solution.py:381
  80.6 6.0 %collective-permute-start.3 = (f32[136,128]{1,0:T(8,128)S(1)}, f32[136,128]{1,0:T(8,128)S(1)}, u32[]{:S(2)}, u32[]{:S(2)}) collective-permute-start(f32[136,128]{1,0:T(8,128)S(1)} %shard_map.126.mine_ref), channel_id=1, source_target_pairs={{0,1},{1,0},{2,3},{3,2},{4,5},{5,4},{6,7},{7,6},{8,9},{9,8},{10,11... | collective-permute-start | bytes 208904 | tf_op jit(solution)/shard_map/ppermute | solution.py:388

commit v3 on v2

--- a/solution.py
+++ b/solution.py
@@ -176,14 +176,14 @@
     source_update(adjoint_of, store, coef_ref, spread_ref, shared, step)
     for b in range(NFREQ // 8):
         edge_ref[8 * b : 8 * b + 8] = edges[b]
-    tile = lax.axis_index("tile")
-
-    @pl.when(tile == 0)
+    odd = lax.axis_index("comp") % 2
+
+    @pl.when(odd == 1)
     def _():
         one_ref[...] = moved_ref[:HALF]
         two_ref[...] = moved_ref[HALF:]
 
-    @pl.when(tile == 1)
+    @pl.when(odd == 0)
     def _():
         one_ref[...] = moved_ref[HALF:]
         two_ref[...] = moved_ref[:HALF]
@@ -195,7 +195,7 @@
 ):
     step = 0
     lane = lane_iota(8)
-    first = jnp.broadcast_to(lax.axis_index("tile"), (8, LANES)) == 0
+    even = jnp.broadcast_to(lax.axis_index("comp") % 2, (8, LANES)) == 0
 
     def propagated(b, p, d):
         rows = slice(8 * b, 8 * b + 8)
@@ -204,7 +204,7 @@
         centre = moved_ref[pl.ds(p * NFREQ + 8 * b, 8), :]
         one = one_ref[pl.ds(at * NFREQ + 8 * b, 8), :]
         two = two_ref[pl.ds(at * NFREQ + 8 * b, 8), :]
-        row = jnp.where(first, one, two) if east else jnp.where(first, two, one)
+        row = jnp.where(even, one, two) if east else jnp.where(even, two, one)
         arrived = edge_ref[rows, p : p + 1]
         if SIN[d] >= 0:
             side, column = RIGHT, jnp.where(lane == LANES - 1, arrived, pltpu.roll(centre, LANES - 1, 1))
@@ -371,13 +371,8 @@
         (f32(NCOMP, LANES), f32(HALF, LANES), f32(HALF, LANES), f32(NFREQ, LANES), f32(8, LANES)),
     )(points, spectrum, coef, spread, vec)
     swap = [(0, 1), (1, 0)]
-    steps = range(comp_count - 1)
-    turns = [
-        [(2 * (i + 1) + t, 2 * i + t) for i in steps] + [(2 * i + 1 - t, 2 * (i + 1) + 1 - t) for i in steps]
-        for t in range(2)
-    ]
-    one = lax.ppermute(one, ("comp", "tile"), turns[0])
-    two = lax.ppermute(two, ("comp", "tile"), turns[1])
+    one = lax.ppermute(one, "comp", [(i, i ^ 1) for i in range(comp_count)])
+    two = lax.ppermute(two, "comp", [(i, ((i + 1) ^ 1) - 1) for i in range(1, comp_count - 1)])
     edge = lax.ppermute(edge, "tile", swap)
     sent = call(
         second_source_kernel, "v" * 11, "v", f32(NX * SENT, LANES), [pltpu.VMEM((NCOMP, LANES), jnp.float32)]

time: 88.6 us -> 84.6 us (0.955)
  starting transfers between devices: 31 us -> 27.4 us
  waiting for transfers between devices: 21.1 us -> 18.6 us
  blocking collectives: 29.1 us -> 31.3 us
    ppermute x2, waiting for transfers between devices: 2.5 us -> 0.01 us  [the longest x1 0.01 us: shards(): one = lax.ppermute(one, 'comp', [(i, i ^ 1) for i in range(comp_count)])]
    ppermute x2, starting transfers between devices: 4.24 us -> 1.75 us  [the longest x1 1.08 us: shards(): one = lax.ppermute(one, 'comp', [(i, i ^ 1) for i in range(comp_count)])]
    all_to_all x1, blocking collectives: 29.1 us -> 31.3 us  [shards(): lax.all_to_all(sent.reshape(NX * SENT, 1, LANES), 'comp', split_axis=0, c...]
    ppermute x1, starting transfers between devices: 5.24 us -> 3.28 us  [shards(): edge = lax.ppermute(edge, 'tile', swap)]
  transfers between devices with their start and end apart: 5 -> 5, of which waited for: 4 -> 3; matrix products, arithmetic and copies ran while one was open for 0% -> 0% of each run, Pallas kernels for 1% -> 1%
where the time goes in v3:
time: 84.6 us; the launch traced here: 84.4 us
  blocking collectives  31.3 us (37%)
  starting transfers between devices  27.4 us (32%)
  waiting for transfers between devices  18.6 us (22%)
  Pallas kernels  6.26 us (7%)
    all_to_all x1, blocking collectives, shards(): lax.all_to_all(sent.reshape(NX * SENT, 1, LANES), 'comp', split_axis=0, c...  31.3 us
    all_to_all x1, waiting for transfers between devices, shards(): lax.all_to_all(by_row.reshape(NCOMP, 1, LANES), 'comp', split_axis=0, con...  16.8 us
    all_to_all x1, starting transfers between devices, shards(): lax.all_to_all(by_row.reshape(NCOMP, 1, LANES), 'comp', split_axis=0, con...  16.3 us
    ppermute x1, starting transfers between devices, shards(): theirs = lax.ppermute(mine, 'tile', swap)  6.01 us
    ppermute x1, starting transfers between devices, shards(): edge = lax.ppermute(edge, 'tile', swap)  3.28 us
    pallas_call x1, Pallas kernels, shards(): call(by_row_kernel, 'h', 'v', f32(NCOMP, LANES), held, WHOLE)(adjoint_final)  2.09 us
  transfers between devices with their start and end apart: 5, of which 3 were waited for; matrix products, arithmetic and copies ran while one was open for 0% of the time, Pallas kernels for 1%

profile of v3, /device:TPU:1, one launch (start us, length us, event | category | flops | bytes accessed | tf_op | source)
XLA Modules:
  0.0 84.4 jit_solution(12603872339892274685)
XLA Ops:
  0.6 0.0 copy-start.4
  0.6 0.0 copy-start.3
  0.7 0.0 copy-start.1
  0.7 0.0 copy-start.9
  0.7 0.0 copy-start.8
  0.7 0.0 copy-start.7
  0.7 0.0 copy-start.2
  0.7 2.1 %shard_map.122 = f32[1152,128]{1,0:T(8,128)} custom-call(f32[9,128,128]{2,1,0:T(8,128)} %in_ref.1), custom_call_target="tpu_custom_call" | custom-call | tf_op jit(solution)/shard_map/pallas_call | solution.py:340
  2.8 16.3 %all-to-all-start = ((f32[1152,1,128]{2,1,0:T(1,128)}), f32[1152,1,128]{2,1,0:T(1,128)S(1)}, u32[]{:S(2)}, u32[]{:S(2)}) async-start(f32[1152,1,128]{2,1,0:T(1,128)} %bitcast.27), calls=%async_computation | async-start | bytes 1179648 | tf_op jit(solution)/shard_map/all_to_all | solution.py:341
  19.3 1.0 %shard_map.123 = (f32[13,32,128]{2,1,0:T(8,128)S(1)}, f32[2,36,128]{2,1,0:T(8,128)S(1)}, f32[8,128]{1,0:T(8,128)S(1)}, f32[2,128,128]{2,1,0:T(8,128)S(1)}, bf16[...) custom-call(f32[2,1152,128]{2,1,0:T(8,128)S(1)} %bitcast.15, f32[2,128]{1,0:T(2,128)S(1)} %bitcast.25, ...), custom_call_target="tpu_custom_call" | custom-call | tf_op jit(solution)/shard_map/pallas_call | solution.py:343
  20.3 16.8 %all-to-all-done = f32[1152,1,128]{2,1,0:T(1,128)S(1)} async-done(((f32[1152,1,128]{2,1,0:T(1,128)}), f32[1152,1,128]{2,1,0:T(1,128)S(1)}, u32[]{:S(2)}, u32[]{:S(2)}) %all-to-all-start) | async-done | bytes 589856 | tf_op jit(solution)/shard_map/all_to_all | solution.py:341
  37.1 0.4 shard_map.124
  37.5 1.1 %collective-permute-start = (f32[576,128]{1,0:T(8,128)S(1)}, f32[576,128]{1,0:T(8,128)S(1)}, u32[]{:S(2)}, u32[]{:S(2)}) collective-permute-start(f32[576,128]{1,0:T(8,128)S(1)} %get-tuple-element.19), channel_id=1, source_target_pairs={{0,2},{2,0},{4,6},{6,4},{8,10},{10,8},{12,14},{14,12},{16,18},{18,... | collective-permute-start | bytes 884744 | tf_op jit(solution)/shard_map/ppermute | solution.py:374
  38.6 0.7 collective-permute-start.1
  39.3 3.3 %collective-permute-start.2 = (f32[32,128]{1,0:T(8,128)S(1)}, f32[32,128]{1,0:T(8,128)S(1)}, u32[]{:S(2)}, u32[]{:S(2)}) collective-permute-start(f32[32,128]{1,0:T(8,128)S(1)} %get-tuple-element.21), channel_id=1, source_target_pairs={{0,1},{1,0},{2,3},{3,2},{4,5},{5,4},{6,7},{7,6},{8,9},{9,8},{10,11... | collective-permute-start | bytes 49160 | tf_op jit(solution)/shard_map/ppermute | solution.py:376
  42.6 0.8 collective-permute-done.2.edge_ref
  43.4 0.0 collective-permute-done.one_ref
  43.4 0.0 collective-permute-done.1.two_ref
  43.4 0.8 shard_map.125
  44.2 31.3 %all_to_all.10 = f32[1280,1,128]{2,1,0:T(1,128)S(1)} all-to-all(f32[1280,1,128]{2,1,0:T(1,128)S(1)} %bitcast.20), channel_id=1, replica_groups=mesh['comp'=128,'tile'=2] {'comp'}, dimensions={0} | all-to-all | bytes 1310720 | tf_op jit(solution)/shard_map/all_to_all | solution.py:380
  75.6 0.2 shard_map.126.mine_ref
  75.8 6.0 %collective-permute-start.3 = (f32[136,128]{1,0:T(8,128)S(1)}, f32[136,128]{1,0:T(8,128)S(1)}, u32[]{:S(2)}, u32[]{:S(2)}) collective-permute-start(f32[136,128]{1,0:T(8,128)S(1)} %shard_map.126.mine_ref), channel_id=1, source_target_pairs={{0,1},{1,0},{2,3},{3,2},{4,5},{5,4},{6,7},{7,6},{8,9},{9,8},{10,11... | collective-permute-start | bytes 208904 | tf_op jit(solution)/shard_map/ppermute | solution.py:383
  81.8 0.9 %collective-permute-done.3.edges_ref = f32[136,128]{1,0:T(8,128)S(1)} collective-permute-done((f32[136,128]{1,0:T(8,128)S(1)}, f32[136,128]{1,0:T(8,128)S(1)}, u32[]{:S(2)}, u32[]{:S(2)}) %collective-permute-start.3) | collective-permute-done | bytes 69664 | tf_op jit(solution)/shard_map/ppermute | solution.py:383
  82.7 1.7 %shard_map.127 = (f32[9,128,128]{2,1,0:T(8,128)}, f32[2,8]{1,0:T(2,128)}) custom-call(f32[1280,128]{1,0:T(8,128)S(1)} %bitcast.19, f32[136,128]{1,0:T(8,128)S(1)} %shard_map.126.mine_ref, f32[136,128]{1,0:T(8,128)S(1)} %collective-permute-done.3.edges_ref, f32[2,128,128]{2,1,0:T(8,128)S(1)} %get-tuple-element.25.face_ref), custom_call_target="tpu_custom_call" | custom-call | tf_op jit(solution)/shard_map/pallas_call | solution.py:384
  (13 shorter events, 0.0 us)
Async XLA Ops:
  0.6 18.6 %copy-start.4 = (f32[4,1,128]{2,1,0:T(1,128)S(1)}, f32[4,1,128]{2,1,0:T(1,128)}, u32[]{:S(2)}) copy-start(f32[4,1,128]{2,1,0:T(1,128)} %param.21) | copy-start | bytes 6148
  0.6 18.6 %copy-start.3 = (s32[4,1,128]{2,1,0:T(1,128)S(1)}, s32[4,1,128]{2,1,0:T(1,128)}, u32[]{:S(2)}) copy-start(s32[4,1,128]{2,1,0:T(1,128)} %param.20) | copy-start | bytes 6148
  0.7 18.6 %copy-start.1 = (s32[128,256]{1,0:T(8,128)S(1)}, s32[128,256]{1,0:T(8,128)}, u32[]{:S(2)}) copy-start(s32[128,256]{1,0:T(8,128)} %mask_ref.1) | copy-start | bytes 393220
  0.7 18.6 %copy-start.9 = (f32[32]{0:T(128)S(1)}, f32[32]{0:T(128)}, u32[]{:S(2)}) copy-start(f32[32]{0:T(128)} %dissip_ref.1) | copy-start | bytes 388
  0.7 18.6 %copy-start.8 = (f32[32]{0:T(128)S(1)}, f32[32]{0:T(128)}, u32[]{:S(2)}) copy-start(f32[32]{0:T(128)} %growth_ref.1) | copy-start | bytes 388
  0.7 18.6 %copy-start.7 = (f32[32]{0:T(128)S(1)}, f32[32]{0:T(128)}, u32[]{:S(2)}) copy-start(f32[32]{0:T(128)} %courant_ref.1) | copy-start | bytes 388
  0.7 18.6 %copy-start.2 = (f32[32,1,128]{2,1,0:T(1,128)S(1)}, f32[32,1,128]{2,1,0:T(1,128)}, u32[]{:S(2)}) copy-start(f32[32,1,128]{2,1,0:T(1,128)} %param.15) | copy-start | bytes 49156
  0.7 18.6 %copy-start.6 = (f32[2,1,128]{2,1,0:T(1,128)S(1)}, f32[2,1,128]{2,1,0:T(1,128)}, u32[]{:S(2)}) copy-start(f32[2,1,128]{2,1,0:T(1,128)} %param.14) | copy-start | bytes 3076
  0.7 18.6 %copy-start.5 = (f32[2,1,128]{2,1,0:T(1,128)S(1)}, f32[2,1,128]{2,1,0:T(1,128)}, u32[]{:S(2)}) copy-start(f32[2,1,128]{2,1,0:T(1,128)} %param.13) | copy-start | bytes 3076
  0.7 18.6 %copy-start = (f32[2,1152,1,128]{3,2,1,0:T(1,128)S(1)}, f32[2,1152,1,128]{3,2,1,0:T(1,128)}, u32[]{:S(2)}) copy-start(f32[2,1152,1,128]{3,2,1,0:T(1,128)} %param.12) | copy-start | bytes 3538948
  2.8 34.3 %all-to-all-start = ((f32[1152,1,128]{2,1,0:T(1,128)}), f32[1152,1,128]{2,1,0:T(1,128)S(1)}, u32[]{:S(2)}, u32[]{:S(2)}) async-start(f32[1152,1,128]{2,1,0:T(1,128)} %bitcast.27), calls=%async_computation | async-start | bytes 1179648 | tf_op jit(solution)/shard_map/all_to_all | solution.py:341
  37.5 5.9 %collective-permute-start = (f32[576,128]{1,0:T(8,128)S(1)}, f32[576,128]{1,0:T(8,128)S(1)}, u32[]{:S(2)}, u32[]{:S(2)}) collective-permute-start(f32[576,128]{1,0:T(8,128)S(1)} %get-tuple-element.19), channel_id=1, source_target_pairs={{0,2},{2,0},{4,6},{6,4},{8,10},{10,8},{12,14},{14,12},{16,18},{18,... | collective-permute-start | bytes 884744 | tf_op jit(solution)/shard_map/ppermute | solution.py:374
  38.6 4.8 %collective-permute-start.1 = (f32[576,128]{1,0:T(8,128)S(1)}, f32[576,128]{1,0:T(8,128)S(1)}, u32[]{:S(2)}, u32[]{:S(2)}) collective-permute-start(f32[576,128]{1,0:T(8,128)S(1)} %get-tuple-element.20), channel_id=1, source_target_pairs={{2,4},{4,2},{6,8},{8,6},{10,12},{12,10},{14,16},{16,14},{18,20},{2... | collective-permute-start | bytes 884744 | tf_op jit(solution)/shard_map/ppermute | solution.py:375
  39.3 4.1 %collective-permute-start.2 = (f32[32,128]{1,0:T(8,128)S(1)}, f32[32,128]{1,0:T(8,128)S(1)}, u32[]{:S(2)}, u32[]{:S(2)}) collective-permute-start(f32[32,128]{1,0:T(8,128)S(1)} %get-tuple-element.21), channel_id=1, source_target_pairs={{0,1},{1,0},{2,3},{3,2},{4,5},{5,4},{6,7},{7,6},{8,9},{9,8},{10,11... | collective-permute-start | bytes 49160 | tf_op jit(solution)/shard_map/ppermute | solution.py:376
  75.8 6.9 %collective-permute-start.3 = (f32[136,128]{1,0:T(8,128)S(1)}, f32[136,128]{1,0:T(8,128)S(1)}, u32[]{:S(2)}, u32[]{:S(2)}) collective-permute-start(f32[136,128]{1,0:T(8,128)S(1)} %shard_map.126.mine_ref), channel_id=1, source_target_pairs={{0,1},{1,0},{2,3},{3,2},{4,5},{5,4},{6,7},{7,6},{8,9},{9,8},{10,11... | collective-permute-start | bytes 208904 | tf_op jit(solution)/shard_map/ppermute | solution.py:383

commit v4 on v3

--- a/solution.py
+++ b/solution.py
@@ -17,6 +17,7 @@
 LOCAL = 9
 QUART = 4
 SENT = LOCAL + 1
+CHUNKS = 2
 CELLS = 16
 
 THETA = np.arange(NDIR) * (2.0 * math.pi / NDIR)
@@ -46,13 +47,22 @@
     return lax.broadcasted_iota(jnp.int32, (rows, LANES), 0)
 
 
-def by_row_kernel(in_ref, out_ref, held_ref, sems):
-    copies = [pltpu.make_async_copy(in_ref.at[j], held_ref.at[j], sems.at[j]) for j in range(LOCAL)]
-    for copy in copies:
-        copy.start()
-    for j, copy in enumerate(copies):
+def by_row_kernel(in_ref, out_ref, held_ref, in_sems, rows_ref, out_sems):
+    count = NX // CHUNKS
+    ins, outs = [], []
+    for c in range(CHUNKS):
+        part = pl.ds(c * count, count)
+        ins.append(pltpu.make_async_copy(in_ref.at[:, part, :], held_ref.at[:, part, :], in_sems.at[c]))
+        part = pl.ds(c * count * LOCAL, count * LOCAL)
+        outs.append(pltpu.make_async_copy(rows_ref.at[part, :], out_ref.at[part, :], out_sems.at[c]))
+        ins[c].start()
+    for c in range(CHUNKS):
+        ins[c].wait()
+        for j in range(LOCAL):
+            rows_ref[pl.ds(c * count * LOCAL + j, count, stride=LOCAL), :] = held_ref[j, c * count : (c + 1) * count]
+        outs[c].start()
+    for copy in outs:
         copy.wait()
-        out_ref[pl.ds(j, NX, stride=LOCAL), :] = held_ref[j]
 
 
 def prepare_kernel(
@@ -337,7 +347,10 @@
     comp_count = lax.axis_size("comp")
     spectrum = background.reshape(NSTEP, NCOMP, LANES)
     held = [pltpu.VMEM((LOCAL, NX, LANES), jnp.float32), pltpu.SemaphoreType.DMA((LOCAL,))]
-    by_row = call(by_row_kernel, "h", "v", f32(NCOMP, LANES), held, WHOLE)(adjoint_final)
+    sems = pltpu.SemaphoreType.DMA((CHUNKS,))
+    by_row = call(
+        by_row_kernel, "h", "h", f32(NCOMP, LANES), [held[0], sems, pltpu.VMEM((NCOMP, LANES), jnp.float32), sems], WHOLE
+    )(adjoint_final)
     points = lax.all_to_all(by_row.reshape(NCOMP, 1, LANES), "comp", split_axis=0, concat_axis=0, tiled=True)
     points = points.reshape(NCOMP, LANES)
     coef, spread, vec, face, owner, cell = call(
@@ -372,7 +385,7 @@
     )(points, spectrum, coef, spread, vec)
     swap = [(0, 1), (1, 0)]
     one = lax.ppermute(one, "comp", [(i, i ^ 1) for i in range(comp_count)])
-    two = lax.ppermute(two, "comp", [(i, ((i + 1) ^ 1) - 1) for i in range(1, comp_count - 1)])
+    two = lax.ppermute(two, "comp", [(i, (((i + 1) ^ 1) - 1) % comp_count) for i in range(comp_count)])
     edge = lax.ppermute(edge, "tile", swap)
     sent = call(
         second_source_kernel, "v" * 11, "v", f32(NX * SENT, LANES), [pltpu.VMEM((NCOMP, LANES), jnp.float32)]

time: 84.6 us -> 82.6 us (0.976)
  blocking collectives: 31.3 us -> 22.8 us
  waiting for transfers between devices: 18.6 us -> 24 us
  starting transfers between devices: 27.4 us -> 28.7 us
    all_to_all x1, blocking collectives: 31.3 us -> 22.8 us  [shards(): lax.all_to_all(sent.reshape(NX * SENT, 1, LANES), 'comp', split_axis=0, c...]
    ppermute x1, waiting for transfers between devices: 0.01 us -> 5.41 us  [shards(): lax.ppermute(two, 'comp', [(i, ((i + 1 ^ 1) - 1) % comp_count) for i in r...]
  transfers between devices with their start and end apart: 5 -> 5, of which waited for: 3 -> 4; matrix products, arithmetic and copies ran while one was open for 0% -> 0% of each run, Pallas kernels for 1% -> 1%
where the time goes in v4:
time: 82.6 us; the launch traced here: 82.4 us
  starting transfers between devices  28.7 us (35%)
  waiting for transfers between devices  24 us (29%)
  blocking collectives  22.8 us (28%)
  Pallas kernels  6.1 us (7%)
  between operations  0.83 us (1%)
    all_to_all x1, blocking collectives, shards(): lax.all_to_all(sent.reshape(NX * SENT, 1, LANES), 'comp', split_axis=0, c...  22.8 us
    all_to_all x1, waiting for transfers between devices, shards(): lax.all_to_all(by_row.reshape(NCOMP, 1, LANES), 'comp', split_axis=0, con...  16.8 us
    all_to_all x1, starting transfers between devices, shards(): lax.all_to_all(by_row.reshape(NCOMP, 1, LANES), 'comp', split_axis=0, con...  16.3 us
    ppermute x1, starting transfers between devices, shards(): theirs = lax.ppermute(mine, 'tile', swap)  6.48 us
    ppermute x1, waiting for transfers between devices, shards(): lax.ppermute(two, 'comp', [(i, ((i + 1 ^ 1) - 1) % comp_count) for i in r...  5.41 us
    ppermute x1, starting transfers between devices, shards(): edge = lax.ppermute(edge, 'tile', swap)  3.62 us
    pallas_call x1, Pallas kernels, shards(): call(by_row_kernel, 'h', 'h', f32(NCOMP, LANES), [held[0], sems, pltpu.VM...  1.93 us
    pallas_call x1, Pallas kernels, shards(): call(last_kernel, 'vvvv', 'hv', (f32(LOCAL, NX, LANES), f32(NSTEP, CELLS...  1.68 us
  transfers between devices with their start and end apart: 5, of which 4 were waited for; matrix products, arithmetic and copies ran while one was open for 0% of the time, Pallas kernels for 1%

profile of v4, /device:TPU:1, one launch (start us, length us, event | category | flops | bytes accessed | tf_op | source)
XLA Modules:
  0.0 82.4 jit_solution(3441140949384363004)
XLA Ops:
  0.6 0.0 copy-start.4
  0.6 0.0 copy-start.3
  0.7 0.0 copy-start.1
  0.7 0.0 copy-start.9
  0.7 0.0 copy-start.8
  0.7 0.0 copy-start.7
  0.7 0.0 copy-start.2
  0.7 1.9 %shard_map.122 = f32[1152,128]{1,0:T(8,128)} custom-call(f32[9,128,128]{2,1,0:T(8,128)} %in_ref.1), custom_call_target="tpu_custom_call" | custom-call | tf_op jit(solution)/shard_map/pallas_call | solution.py:351
  2.7 16.3 %all-to-all-start = ((f32[1152,1,128]{2,1,0:T(1,128)}), f32[1152,1,128]{2,1,0:T(1,128)S(1)}, u32[]{:S(2)}, u32[]{:S(2)}) async-start(f32[1152,1,128]{2,1,0:T(1,128)} %bitcast.27), calls=%async_computation | async-start | bytes 1179648 | tf_op jit(solution)/shard_map/all_to_all | solution.py:354
  19.1 1.0 %shard_map.123 = (f32[13,32,128]{2,1,0:T(8,128)S(1)}, f32[2,36,128]{2,1,0:T(8,128)S(1)}, f32[8,128]{1,0:T(8,128)S(1)}, f32[2,128,128]{2,1,0:T(8,128)S(1)}, bf16[...) custom-call(f32[2,1152,128]{2,1,0:T(8,128)S(1)} %bitcast.15, f32[2,128]{1,0:T(2,128)S(1)} %bitcast.25, ...), custom_call_target="tpu_custom_call" | custom-call | tf_op jit(solution)/shard_map/pallas_call | solution.py:356
  20.1 16.8 %all-to-all-done = f32[1152,1,128]{2,1,0:T(1,128)S(1)} async-done(((f32[1152,1,128]{2,1,0:T(1,128)}), f32[1152,1,128]{2,1,0:T(1,128)S(1)}, u32[]{:S(2)}, u32[]{:S(2)}) %all-to-all-start) | async-done | bytes 589856 | tf_op jit(solution)/shard_map/all_to_all | solution.py:354
  37.0 0.4 shard_map.124
  37.4 1.1 %collective-permute-start = (f32[576,128]{1,0:T(8,128)S(1)}, f32[576,128]{1,0:T(8,128)S(1)}, u32[]{:S(2)}, u32[]{:S(2)}) collective-permute-start(f32[576,128]{1,0:T(8,128)S(1)} %get-tuple-element.19), channel_id=1, source_target_pairs={{0,2},{2,0},{4,6},{6,4},{8,10},{10,8},{12,14},{14,12},{16,18},{18,... | collective-permute-start | bytes 884744 | tf_op jit(solution)/shard_map/ppermute | solution.py:387
  38.4 1.1 %collective-permute-start.1 = (f32[576,128]{1,0:T(8,128)S(1)}, f32[576,128]{1,0:T(8,128)S(1)}, u32[]{:S(2)}, u32[]{:S(2)}) collective-permute-start(f32[576,128]{1,0:T(8,128)S(1)} %get-tuple-element.20), channel_id=1, source_target_pairs={{0,254},{2,4},{4,2},{6,8},{8,6},{10,12},{12,10},{14,16},{16,14},{1... | collective-permute-start | bytes 884744 | tf_op jit(solution)/shard_map/ppermute | solution.py:388
  39.6 3.6 %collective-permute-start.2 = (f32[32,128]{1,0:T(8,128)S(1)}, f32[32,128]{1,0:T(8,128)S(1)}, u32[]{:S(2)}, u32[]{:S(2)}) collective-permute-start(f32[32,128]{1,0:T(8,128)S(1)} %get-tuple-element.21), channel_id=1, source_target_pairs={{0,1},{1,0},{2,3},{3,2},{4,5},{5,4},{6,7},{7,6},{8,9},{9,8},{10,11... | collective-permute-start | bytes 49160 | tf_op jit(solution)/shard_map/ppermute | solution.py:389
  43.2 0.8 %collective-permute-done.2.edge_ref = f32[32,128]{1,0:T(8,128)S(1)} collective-permute-done((f32[32,128]{1,0:T(8,128)S(1)}, f32[32,128]{1,0:T(8,128)S(1)}, u32[]{:S(2)}, u32[]{:S(2)}) %collective-permute-start.2) | collective-permute-done | bytes 16416 | tf_op jit(solution)/shard_map/ppermute | solution.py:389
  44.0 0.0 collective-permute-done.one_ref
  44.0 5.4 %collective-permute-done.1.two_ref = f32[576,128]{1,0:T(8,128)S(1)} collective-permute-done((f32[576,128]{1,0:T(8,128)S(1)}, f32[576,128]{1,0:T(8,128)S(1)}, u32[]{:S(2)}, u32[]{:S(2)}) %collective-permute-start.1) | collective-permute-done | bytes 294944 | tf_op jit(solution)/shard_map/ppermute | solution.py:388
  49.5 0.8 shard_map.125
  50.3 22.8 %all_to_all.10 = f32[1280,1,128]{2,1,0:T(1,128)S(1)} all-to-all(f32[1280,1,128]{2,1,0:T(1,128)S(1)} %bitcast.20), channel_id=1, replica_groups=mesh['comp'=128,'tile'=2] {'comp'}, dimensions={0} | all-to-all | bytes 1310720 | tf_op jit(solution)/shard_map/all_to_all | solution.py:393
  73.1 0.2 shard_map.126.mine_ref
  73.4 6.5 %collective-permute-start.3 = (f32[136,128]{1,0:T(8,128)S(1)}, f32[136,128]{1,0:T(8,128)S(1)}, u32[]{:S(2)}, u32[]{:S(2)}) collective-permute-start(f32[136,128]{1,0:T(8,128)S(1)} %shard_map.126.mine_ref), channel_id=1, source_target_pairs={{0,1},{1,0},{2,3},{3,2},{4,5},{5,4},{6,7},{7,6},{8,9},{9,8},{10,11... | collective-permute-start | bytes 208904 | tf_op jit(solution)/shard_map/ppermute | solution.py:396
  79.8 0.9 %collective-permute-done.3.edges_ref = f32[136,128]{1,0:T(8,128)S(1)} collective-permute-done((f32[136,128]{1,0:T(8,128)S(1)}, f32[136,128]{1,0:T(8,128)S(1)}, u32[]{:S(2)}, u32[]{:S(2)}) %collective-permute-start.3) | collective-permute-done | bytes 69664 | tf_op jit(solution)/shard_map/ppermute | solution.py:396
  80.7 1.7 %shard_map.127 = (f32[9,128,128]{2,1,0:T(8,128)}, f32[2,8]{1,0:T(2,128)}) custom-call(f32[1280,128]{1,0:T(8,128)S(1)} %bitcast.19, f32[136,128]{1,0:T(8,128)S(1)} %shard_map.126.mine_ref, f32[136,128]{1,0:T(8,128)S(1)} %collective-permute-done.3.edges_ref, f32[2,128,128]{2,1,0:T(8,128)S(1)} %get-tuple-element.25.face_ref), custom_call_target="tpu_custom_call" | custom-call | tf_op jit(solution)/shard_map/pallas_call | solution.py:397
  (13 shorter events, 0.0 us)
Async XLA Ops:
  0.6 18.4 %copy-start.4 = (f32[4,1,128]{2,1,0:T(1,128)S(1)}, f32[4,1,128]{2,1,0:T(1,128)}, u32[]{:S(2)}) copy-start(f32[4,1,128]{2,1,0:T(1,128)} %param.21) | copy-start | bytes 6148
  0.6 18.4 %copy-start.3 = (s32[4,1,128]{2,1,0:T(1,128)S(1)}, s32[4,1,128]{2,1,0:T(1,128)}, u32[]{:S(2)}) copy-start(s32[4,1,128]{2,1,0:T(1,128)} %param.20) | copy-start | bytes 6148
  0.7 18.4 %copy-start.1 = (s32[128,256]{1,0:T(8,128)S(1)}, s32[128,256]{1,0:T(8,128)}, u32[]{:S(2)}) copy-start(s32[128,256]{1,0:T(8,128)} %mask_ref.1) | copy-start | bytes 393220
  0.7 18.4 %copy-start.9 = (f32[32]{0:T(128)S(1)}, f32[32]{0:T(128)}, u32[]{:S(2)}) copy-start(f32[32]{0:T(128)} %dissip_ref.1) | copy-start | bytes 388
  0.7 18.4 %copy-start.8 = (f32[32]{0:T(128)S(1)}, f32[32]{0:T(128)}, u32[]{:S(2)}) copy-start(f32[32]{0:T(128)} %growth_ref.1) | copy-start | bytes 388
  0.7 18.4 %copy-start.7 = (f32[32]{0:T(128)S(1)}, f32[32]{0:T(128)}, u32[]{:S(2)}) copy-start(f32[32]{0:T(128)} %courant_ref.1) | copy-start | bytes 388
  0.7 18.4 %copy-start.2 = (f32[32,1,128]{2,1,0:T(1,128)S(1)}, f32[32,1,128]{2,1,0:T(1,128)}, u32[]{:S(2)}) copy-start(f32[32,1,128]{2,1,0:T(1,128)} %param.15) | copy-start | bytes 49156
  0.7 18.4 %copy-start.6 = (f32[2,1,128]{2,1,0:T(1,128)S(1)}, f32[2,1,128]{2,1,0:T(1,128)}, u32[]{:S(2)}) copy-start(f32[2,1,128]{2,1,0:T(1,128)} %param.14) | copy-start | bytes 3076
  0.7 18.4 %copy-start.5 = (f32[2,1,128]{2,1,0:T(1,128)S(1)}, f32[2,1,128]{2,1,0:T(1,128)}, u32[]{:S(2)}) copy-start(f32[2,1,128]{2,1,0:T(1,128)} %param.13) | copy-start | bytes 3076
  0.7 18.4 %copy-start = (f32[2,1152,1,128]{3,2,1,0:T(1,128)S(1)}, f32[2,1152,1,128]{3,2,1,0:T(1,128)}, u32[]{:S(2)}) copy-start(f32[2,1152,1,128]{3,2,1,0:T(1,128)} %param.12) | copy-start | bytes 3538948
  2.7 34.3 %all-to-all-start = ((f32[1152,1,128]{2,1,0:T(1,128)}), f32[1152,1,128]{2,1,0:T(1,128)S(1)}, u32[]{:S(2)}, u32[]{:S(2)}) async-start(f32[1152,1,128]{2,1,0:T(1,128)} %bitcast.27), calls=%async_computation | async-start | bytes 1179648 | tf_op jit(solution)/shard_map/all_to_all | solution.py:354
  37.4 6.7 %collective-permute-start = (f32[576,128]{1,0:T(8,128)S(1)}, f32[576,128]{1,0:T(8,128)S(1)}, u32[]{:S(2)}, u32[]{:S(2)}) collective-permute-start(f32[576,128]{1,0:T(8,128)S(1)} %get-tuple-element.19), channel_id=1, source_target_pairs={{0,2},{2,0},{4,6},{6,4},{8,10},{10,8},{12,14},{14,12},{16,18},{18,... | collective-permute-start | bytes 884744 | tf_op jit(solution)/shard_map/ppermute | solution.py:387
  38.4 11.0 %collective-permute-start.1 = (f32[576,128]{1,0:T(8,128)S(1)}, f32[576,128]{1,0:T(8,128)S(1)}, u32[]{:S(2)}, u32[]{:S(2)}) collective-permute-start(f32[576,128]{1,0:T(8,128)S(1)} %get-tuple-element.20), channel_id=1, source_target_pairs={{0,254},{2,4},{4,2},{6,8},{8,6},{10,12},{12,10},{14,16},{16,14},{1... | collective-permute-start | bytes 884744 | tf_op jit(solution)/shard_map/ppermute | solution.py:388
  39.6 4.5 %collective-permute-start.2 = (f32[32,128]{1,0:T(8,128)S(1)}, f32[32,128]{1,0:T(8,128)S(1)}, u32[]{:S(2)}, u32[]{:S(2)}) collective-permute-start(f32[32,128]{1,0:T(8,128)S(1)} %get-tuple-element.21), channel_id=1, source_target_pairs={{0,1},{1,0},{2,3},{3,2},{4,5},{5,4},{6,7},{7,6},{8,9},{9,8},{10,11... | collective-permute-start | bytes 49160 | tf_op jit(solution)/shard_map/ppermute | solution.py:389
  73.4 7.4 %collective-permute-start.3 = (f32[136,128]{1,0:T(8,128)S(1)}, f32[136,128]{1,0:T(8,128)S(1)}, u32[]{:S(2)}, u32[]{:S(2)}) collective-permute-start(f32[136,128]{1,0:T(8,128)S(1)} %shard_map.126.mine_ref), channel_id=1, source_target_pairs={{0,1},{1,0},{2,3},{3,2},{4,5},{5,4},{6,7},{7,6},{8,9},{9,8},{10,11... | collective-permute-start | bytes 208904 | tf_op jit(solution)/shard_map/ppermute | solution.py:396

commit v5 on v4

--- a/solution.py
+++ b/solution.py
@@ -384,8 +384,11 @@
         (f32(NCOMP, LANES), f32(HALF, LANES), f32(HALF, LANES), f32(NFREQ, LANES), f32(8, LANES)),
     )(points, spectrum, coef, spread, vec)
     swap = [(0, 1), (1, 0)]
+    last = comp_count - 1
+    pairs = [(2 * i + t, 2 * (((i + 1) ^ 1) - 1) + t) for i in range(1, last) for t in range(2)]
+    pairs += [(2 * i + t, 2 * i + 1 - t) for i in (0, last) for t in range(2)]
     one = lax.ppermute(one, "comp", [(i, i ^ 1) for i in range(comp_count)])
-    two = lax.ppermute(two, "comp", [(i, (((i + 1) ^ 1) - 1) % comp_count) for i in range(comp_count)])
+    two = lax.ppermute(two, ("comp", "tile"), pairs)
     edge = lax.ppermute(edge, "tile", swap)
     sent = call(
         second_source_kernel, "v" * 11, "v", f32(NX * SENT, LANES), [pltpu.VMEM((NCOMP, LANES), jnp.float32)]

time: 82.6 us -> 82.6 us (level)
  blocking collectives: 22.8 us -> 29.9 us
  waiting for transfers between devices: 24 us -> 19.1 us
  starting transfers between devices: 28.7 us -> 26.5 us
    all_to_all x1, blocking collectives: 22.8 us -> 29.9 us  [shards(): lax.all_to_all(sent.reshape(NX * SENT, 1, LANES), 'comp', split_axis=0, c...]
    ppermute x1, waiting for transfers between devices: 5.41 us -> 0.01 us  [shards(): two = lax.ppermute(two, ('comp', 'tile'), pairs)]
    ppermute x1, starting transfers between devices: 3.62 us -> 0.01 us  [shards(): edge = lax.ppermute(edge, 'tile', swap)]
    ppermute x1, starting transfers between devices: 1.12 us -> 3.19 us  [shards(): two = lax.ppermute(two, ('comp', 'tile'), pairs)]
where the time goes in v5:
time: 82.6 us; the launch traced here: 82.4 us
  blocking collectives  29.9 us (36%)
  starting transfers between devices  26.5 us (32%)
  waiting for transfers between devices  19.1 us (23%)
  Pallas kernels  6.1 us (7%)
  between operations  0.83 us (1%)
    all_to_all x1, blocking collectives, shards(): lax.all_to_all(sent.reshape(NX * SENT, 1, LANES), 'comp', split_axis=0, c...  29.9 us
    all_to_all x1, waiting for transfers between devices, shards(): lax.all_to_all(by_row.reshape(NCOMP, 1, LANES), 'comp', split_axis=0, con...  16.8 us
    all_to_all x1, starting transfers between devices, shards(): lax.all_to_all(by_row.reshape(NCOMP, 1, LANES), 'comp', split_axis=0, con...  16.3 us
    ppermute x1, starting transfers between devices, shards(): theirs = lax.ppermute(mine, 'tile', swap)  5.87 us
    ppermute x1, starting transfers between devices, shards(): two = lax.ppermute(two, ('comp', 'tile'), pairs)  3.19 us
    pallas_call x1, Pallas kernels, shards(): call(by_row_kernel, 'h', 'h', f32(NCOMP, LANES), [held[0], sems, pltpu.VM...  1.93 us
    pallas_call x1, Pallas kernels, shards(): call(last_kernel, 'vvvv', 'hv', (f32(LOCAL, NX, LANES), f32(NSTEP, CELLS...  1.68 us
  transfers between devices with their start and end apart: 5, of which 4 were waited for; matrix products, arithmetic and copies ran while one was open for 0% of the time, Pallas kernels for 1%

profile of v5, /device:TPU:1, one launch (start us, length us, event | category | flops | bytes accessed | tf_op | source)
XLA Modules:
  0.0 82.4 jit_solution(6398841331291086715)
XLA Ops:
  0.6 0.0 copy-start.4
  0.6 0.0 copy-start.3
  0.7 0.0 copy-start.1
  0.7 0.0 copy-start.9
  0.7 0.0 copy-start.8
  0.7 0.0 copy-start.7
  0.7 0.0 copy-start.2
  0.7 1.9 %shard_map.122 = f32[1152,128]{1,0:T(8,128)} custom-call(f32[9,128,128]{2,1,0:T(8,128)} %in_ref.1), custom_call_target="tpu_custom_call" | custom-call | tf_op jit(solution)/shard_map/pallas_call | solution.py:351
  2.7 16.3 %all-to-all-start = ((f32[1152,1,128]{2,1,0:T(1,128)}), f32[1152,1,128]{2,1,0:T(1,128)S(1)}, u32[]{:S(2)}, u32[]{:S(2)}) async-start(f32[1152,1,128]{2,1,0:T(1,128)} %bitcast.27), calls=%async_computation | async-start | bytes 1179648 | tf_op jit(solution)/shard_map/all_to_all | solution.py:354
  19.1 1.0 %shard_map.123 = (f32[13,32,128]{2,1,0:T(8,128)S(1)}, f32[2,36,128]{2,1,0:T(8,128)S(1)}, f32[8,128]{1,0:T(8,128)S(1)}, f32[2,128,128]{2,1,0:T(8,128)S(1)}, bf16[...) custom-call(f32[2,1152,128]{2,1,0:T(8,128)S(1)} %bitcast.15, f32[2,128]{1,0:T(2,128)S(1)} %bitcast.25, ...), custom_call_target="tpu_custom_call" | custom-call | tf_op jit(solution)/shard_map/pallas_call | solution.py:356
  20.1 16.8 %all-to-all-done = f32[1152,1,128]{2,1,0:T(1,128)S(1)} async-done(((f32[1152,1,128]{2,1,0:T(1,128)}), f32[1152,1,128]{2,1,0:T(1,128)S(1)}, u32[]{:S(2)}, u32[]{:S(2)}) %all-to-all-start) | async-done | bytes 589856 | tf_op jit(solution)/shard_map/all_to_all | solution.py:354
  37.0 0.4 shard_map.124
  37.4 1.1 %collective-permute-start = (f32[576,128]{1,0:T(8,128)S(1)}, f32[576,128]{1,0:T(8,128)S(1)}, u32[]{:S(2)}, u32[]{:S(2)}) collective-permute-start(f32[576,128]{1,0:T(8,128)S(1)} %get-tuple-element.19), channel_id=1, source_target_pairs={{0,2},{2,0},{4,6},{6,4},{8,10},{10,8},{12,14},{14,12},{16,18},{18,... | collective-permute-start | bytes 884744 | tf_op jit(solution)/shard_map/ppermute | solution.py:390
  38.4 3.2 %collective-permute-start.1 = (f32[576,128]{1,0:T(8,128)S(1)}, f32[576,128]{1,0:T(8,128)S(1)}, u32[]{:S(2)}, u32[]{:S(2)}) collective-permute-start(f32[576,128]{1,0:T(8,128)S(1)} %get-tuple-element.20), channel_id=1, source_target_pairs={{2,4},{3,5},{4,2},{5,3},{6,8},{7,9},{8,6},{9,7},{10,12},{11,13},{1... | collective-permute-start | bytes 884744 | tf_op jit(solution)/shard_map/ppermute | solution.py:391
  41.6 0.0 collective-permute-start.2
  41.6 1.2 %collective-permute-done.2.edge_ref = f32[32,128]{1,0:T(8,128)S(1)} collective-permute-done((f32[32,128]{1,0:T(8,128)S(1)}, f32[32,128]{1,0:T(8,128)S(1)}, u32[]{:S(2)}, u32[]{:S(2)}) %collective-permute-start.2) | collective-permute-done | bytes 16416 | tf_op jit(solution)/shard_map/ppermute | solution.py:392
  42.9 0.2 collective-permute-done.one_ref
  43.0 0.0 collective-permute-done.1.two_ref
  43.0 0.8 shard_map.125
  43.9 29.9 %all_to_all.10 = f32[1280,1,128]{2,1,0:T(1,128)S(1)} all-to-all(f32[1280,1,128]{2,1,0:T(1,128)S(1)} %bitcast.20), channel_id=1, replica_groups=mesh['comp'=128,'tile'=2] {'comp'}, dimensions={0} | all-to-all | bytes 1310720 | tf_op jit(solution)/shard_map/all_to_all | solution.py:396
  73.7 0.2 shard_map.126.mine_ref
  74.0 5.9 %collective-permute-start.3 = (f32[136,128]{1,0:T(8,128)S(1)}, f32[136,128]{1,0:T(8,128)S(1)}, u32[]{:S(2)}, u32[]{:S(2)}) collective-permute-start(f32[136,128]{1,0:T(8,128)S(1)} %shard_map.126.mine_ref), channel_id=1, source_target_pairs={{0,1},{1,0},{2,3},{3,2},{4,5},{5,4},{6,7},{7,6},{8,9},{9,8},{10,11... | collective-permute-start | bytes 208904 | tf_op jit(solution)/shard_map/ppermute | solution.py:399
  79.8 0.9 %collective-permute-done.3.edges_ref = f32[136,128]{1,0:T(8,128)S(1)} collective-permute-done((f32[136,128]{1,0:T(8,128)S(1)}, f32[136,128]{1,0:T(8,128)S(1)}, u32[]{:S(2)}, u32[]{:S(2)}) %collective-permute-start.3) | collective-permute-done | bytes 69664 | tf_op jit(solution)/shard_map/ppermute | solution.py:399
  80.7 1.7 %shard_map.127 = (f32[9,128,128]{2,1,0:T(8,128)}, f32[2,8]{1,0:T(2,128)}) custom-call(f32[1280,128]{1,0:T(8,128)S(1)} %bitcast.19, f32[136,128]{1,0:T(8,128)S(1)} %shard_map.126.mine_ref, f32[136,128]{1,0:T(8,128)S(1)} %collective-permute-done.3.edges_ref, f32[2,128,128]{2,1,0:T(8,128)S(1)} %get-tuple-element.25.face_ref), custom_call_target="tpu_custom_call" | custom-call | tf_op jit(solution)/shard_map/pallas_call | solution.py:400
  (13 shorter events, 0.0 us)
Async XLA Ops:
  0.6 18.4 %copy-start.4 = (f32[4,1,128]{2,1,0:T(1,128)S(1)}, f32[4,1,128]{2,1,0:T(1,128)}, u32[]{:S(2)}) copy-start(f32[4,1,128]{2,1,0:T(1,128)} %param.21) | copy-start | bytes 6148
  0.6 18.4 %copy-start.3 = (s32[4,1,128]{2,1,0:T(1,128)S(1)}, s32[4,1,128]{2,1,0:T(1,128)}, u32[]{:S(2)}) copy-start(s32[4,1,128]{2,1,0:T(1,128)} %param.20) | copy-start | bytes 6148
  0.7 18.4 %copy-start.1 = (s32[128,256]{1,0:T(8,128)S(1)}, s32[128,256]{1,0:T(8,128)}, u32[]{:S(2)}) copy-start(s32[128,256]{1,0:T(8,128)} %mask_ref.1) | copy-start | bytes 393220
  0.7 18.4 %copy-start.9 = (f32[32]{0:T(128)S(1)}, f32[32]{0:T(128)}, u32[]{:S(2)}) copy-start(f32[32]{0:T(128)} %dissip_ref.1) | copy-start | bytes 388
  0.7 18.4 %copy-start.8 = (f32[32]{0:T(128)S(1)}, f32[32]{0:T(128)}, u32[]{:S(2)}) copy-start(f32[32]{0:T(128)} %growth_ref.1) | copy-start | bytes 388
  0.7 18.4 %copy-start.7 = (f32[32]{0:T(128)S(1)}, f32[32]{0:T(128)}, u32[]{:S(2)}) copy-start(f32[32]{0:T(128)} %courant_ref.1) | copy-start | bytes 388
  0.7 18.4 %copy-start.2 = (f32[32,1,128]{2,1,0:T(1,128)S(1)}, f32[32,1,128]{2,1,0:T(1,128)}, u32[]{:S(2)}) copy-start(f32[32,1,128]{2,1,0:T(1,128)} %param.15) | copy-start | bytes 49156
  0.7 18.4 %copy-start.6 = (f32[2,1,128]{2,1,0:T(1,128)S(1)}, f32[2,1,128]{2,1,0:T(1,128)}, u32[]{:S(2)}) copy-start(f32[2,1,128]{2,1,0:T(1,128)} %param.14) | copy-start | bytes 3076
  0.7 18.4 %copy-start.5 = (f32[2,1,128]{2,1,0:T(1,128)S(1)}, f32[2,1,128]{2,1,0:T(1,128)}, u32[]{:S(2)}) copy-start(f32[2,1,128]{2,1,0:T(1,128)} %param.13) | copy-start | bytes 3076
  0.7 18.4 %copy-start = (f32[2,1152,1,128]{3,2,1,0:T(1,128)S(1)}, f32[2,1152,1,128]{3,2,1,0:T(1,128)}, u32[]{:S(2)}) copy-start(f32[2,1152,1,128]{3,2,1,0:T(1,128)} %param.12) | copy-start | bytes 3538948
  2.7 34.3 %all-to-all-start = ((f32[1152,1,128]{2,1,0:T(1,128)}), f32[1152,1,128]{2,1,0:T(1,128)S(1)}, u32[]{:S(2)}, u32[]{:S(2)}) async-start(f32[1152,1,128]{2,1,0:T(1,128)} %bitcast.27), calls=%async_computation | async-start | bytes 1179648 | tf_op jit(solution)/shard_map/all_to_all | solution.py:354
  37.4 5.7 %collective-permute-start = (f32[576,128]{1,0:T(8,128)S(1)}, f32[576,128]{1,0:T(8,128)S(1)}, u32[]{:S(2)}, u32[]{:S(2)}) collective-permute-start(f32[576,128]{1,0:T(8,128)S(1)} %get-tuple-element.19), channel_id=1, source_target_pairs={{0,2},{2,0},{4,6},{6,4},{8,10},{10,8},{12,14},{14,12},{16,18},{18,... | collective-permute-start | bytes 884744 | tf_op jit(solution)/shard_map/ppermute | solution.py:390
  38.4 4.6 %collective-permute-start.1 = (f32[576,128]{1,0:T(8,128)S(1)}, f32[576,128]{1,0:T(8,128)S(1)}, u32[]{:S(2)}, u32[]{:S(2)}) collective-permute-start(f32[576,128]{1,0:T(8,128)S(1)} %get-tuple-element.20), channel_id=1, source_target_pairs={{2,4},{3,5},{4,2},{5,3},{6,8},{7,9},{8,6},{9,7},{10,12},{11,13},{1... | collective-permute-start | bytes 884744 | tf_op jit(solution)/shard_map/ppermute | solution.py:391
  41.6 1.2 %collective-permute-start.2 = (f32[32,128]{1,0:T(8,128)S(1)}, f32[32,128]{1,0:T(8,128)S(1)}, u32[]{:S(2)}, u32[]{:S(2)}) collective-permute-start(f32[32,128]{1,0:T(8,128)S(1)} %get-tuple-element.21), channel_id=1, source_target_pairs={{0,1},{1,0},{2,3},{3,2},{4,5},{5,4},{6,7},{7,6},{8,9},{9,8},{10,11... | collective-permute-start | bytes 49160 | tf_op jit(solution)/shard_map/ppermute | solution.py:392
  74.0 6.8 %collective-permute-start.3 = (f32[136,128]{1,0:T(8,128)S(1)}, f32[136,128]{1,0:T(8,128)S(1)}, u32[]{:S(2)}, u32[]{:S(2)}) collective-permute-start(f32[136,128]{1,0:T(8,128)S(1)} %shard_map.126.mine_ref), channel_id=1, source_target_pairs={{0,1},{1,0},{2,3},{3,2},{4,5},{5,4},{6,7},{7,6},{8,9},{9,8},{10,11... | collective-permute-start | bytes 208904 | tf_op jit(solution)/shard_map/ppermute | solution.py:399

commit v6 on v5

--- a/solution.py
+++ b/solution.py
@@ -199,36 +199,67 @@
         two_ref[...] = moved_ref[:HALF]
 
 
+def propagate_half(east, moved_ref, near_ref, edge_ref, spectrum_ref, coef_ref, spread_ref, half_ref, sums_ref):
+    step = 0
+    lane = lane_iota(8)
+    half = NDIR // 2
+    face, start = (UP, 0) if east else (DOWN, half)
+    damped = jnp.zeros((8, LANES), jnp.float32)
+    stress = jnp.zeros((8, LANES), jnp.float32)
+    for b in range(NFREQ // 8):
+        rows = slice(8 * b, 8 * b + 8)
+        plain = jnp.zeros((8, LANES), jnp.float32)
+        spread = jnp.zeros((8, LANES), jnp.float32)
+        for at in range(half):
+            p = start + at
+            d = ORDER[p]
+            centre = moved_ref[pl.ds(p * NFREQ + 8 * b, 8), :]
+            row = near_ref[pl.ds(at * NFREQ + 8 * b, 8), :]
+            arrived = edge_ref[rows, p : p + 1]
+            if SIN[d] >= 0:
+                side, column = RIGHT, jnp.where(lane == LANES - 1, arrived, pltpu.roll(centre, LANES - 1, 1))
+            else:
+                side, column = LEFT, jnp.where(lane == 0, arrived, pltpu.roll(centre, 1, 1))
+            value = (
+                centre
+                + abs(COS[d]) * (coef_ref[face, rows] * (row - centre))
+                + abs(SIN[d]) * (coef_ref[side, rows] * (column - centre))
+            )
+            half_ref[pl.ds(at * NFREQ + 8 * b, 8), :] = value
+            product = spectrum_ref[step, pl.ds(8 * b * NDIR + d, 8, stride=NDIR), :] * value
+            plain = plain + product
+            spread = spread + spread_ref[step, d : d + 1, :] * product
+        damped = damped + coef_ref[DISSIP, rows] * plain
+        stress = stress + coef_ref[GROWTH, rows] * spread
+    sums_ref[:8] = damped
+    sums_ref[8:] = stress
+
+
+def first_half_kernel(moved_ref, one_ref, edge_ref, spectrum_ref, coef_ref, spread_ref, half_ref, sums_ref):
+    odd = lax.axis_index("comp") % 2
+    for parity, east in ((0, True), (1, False)):
+
+        @pl.when(odd == parity)
+        def _():
+            propagate_half(east, moved_ref, one_ref, edge_ref, spectrum_ref, coef_ref, spread_ref, half_ref, sums_ref)
+
+
 def second_source_kernel(
-    moved_ref, one_ref, two_ref, edge_ref, spectrum_ref, coef_ref, spread_ref, vec_ref, stress_ref,
-    owner_ref, cell_ref, out_ref, held_ref,
+    moved_ref, two_ref, edge_ref, spectrum_ref, coef_ref, spread_ref, vec_ref, stress_ref,
+    owner_ref, cell_ref, done_ref, done_sums_ref, out_ref, half_ref, sums_ref,
 ):
     step = 0
-    lane = lane_iota(8)
-    even = jnp.broadcast_to(lax.axis_index("comp") % 2, (8, LANES)) == 0
-
-    def propagated(b, p, d):
-        rows = slice(8 * b, 8 * b + 8)
-        east = p < NDIR // 2
-        face, at = (UP, p) if east else (DOWN, p - NDIR // 2)
-        centre = moved_ref[pl.ds(p * NFREQ + 8 * b, 8), :]
-        one = one_ref[pl.ds(at * NFREQ + 8 * b, 8), :]
-        two = two_ref[pl.ds(at * NFREQ + 8 * b, 8), :]
-        row = jnp.where(even, one, two) if east else jnp.where(even, two, one)
-        arrived = edge_ref[rows, p : p + 1]
-        if SIN[d] >= 0:
-            side, column = RIGHT, jnp.where(lane == LANES - 1, arrived, pltpu.roll(centre, LANES - 1, 1))
-        else:
-            side, column = LEFT, jnp.where(lane == 0, arrived, pltpu.roll(centre, 1, 1))
-        value = (
-            centre
-            + abs(COS[d]) * (coef_ref[face, rows] * (row - centre))
-            + abs(SIN[d]) * (coef_ref[side, rows] * (column - centre))
-        )
-        held_ref[pl.ds(p * NFREQ + 8 * b, 8), :] = value
-        return value
-
-    shared, stress = source_sums(propagated, spectrum_ref, coef_ref, spread_ref, vec_ref, step)
+    odd = lax.axis_index("comp") % 2
+    even = jnp.broadcast_to(odd, (8, LANES)) == 0
+    for parity, east in ((0, False), (1, True)):
+
+        @pl.when(odd == parity)
+        def _():
+            propagate_half(east, moved_ref, two_ref, edge_ref, spectrum_ref, coef_ref, spread_ref, half_ref, sums_ref)
+
+    damped = jnp.sum(done_sums_ref[:8] + sums_ref[:8], axis=0, keepdims=True)
+    stress = jnp.sum(done_sums_ref[8:] + sums_ref[8:], axis=0, keepdims=True)
+    shared, stress = vec_ref[step : step + 1] * damped, vec_ref[2:3] * stress
 
     values = jnp.concatenate(
         [
@@ -248,7 +279,10 @@
     out_ref[pl.ds(LOCAL, NX, stride=SENT), :] = cells
 
     def adjoint_of(b, p, d):
-        return held_ref[pl.ds(p * NFREQ + 8 * b, 8), :]
+        east = p < NDIR // 2
+        rows = pl.ds((p if east else p - NDIR // 2) * NFREQ + 8 * b, 8)
+        done, here = done_ref[rows, :], half_ref[rows, :]
+        return jnp.where(even, done, here) if east else jnp.where(even, here, done)
 
     def store(b, p, d, value):
         at = 8 * b * QUART * SENT + d // LOCAL * SENT + d % LOCAL
@@ -390,9 +424,16 @@
     one = lax.ppermute(one, "comp", [(i, i ^ 1) for i in range(comp_count)])
     two = lax.ppermute(two, ("comp", "tile"), pairs)
     edge = lax.ppermute(edge, "tile", swap)
+    done, done_sums = call(first_half_kernel, "v" * 6, "vv", (f32(HALF, LANES), f32(16, LANES)))(
+        moved, one, edge, spectrum, coef, spread
+    )
     sent = call(
-        second_source_kernel, "v" * 11, "v", f32(NX * SENT, LANES), [pltpu.VMEM((NCOMP, LANES), jnp.float32)]
-    )(moved, one, two, edge, spectrum, coef, spread, vec, stress, owner, cell)
+        second_source_kernel,
+        "v" * 12,
+        "v",
+        f32(NX * SENT, LANES),
+        [pltpu.VMEM((HALF, LANES), jnp.float32), pltpu.VMEM((16, LANES), jnp.float32)],
+    )(moved, two, edge, spectrum, coef, spread, vec, stress, owner, cell, done, done_sums)
     arrived = lax.all_to_all(sent.reshape(NX * SENT, 1, LANES), "comp", split_axis=0, concat_axis=0, tiled=True)
     arrived = arrived.reshape(NX * SENT, LANES)
     mine = call(edges_kernel, "v", "v", f32(NX + 8, LANES))(arrived)

time: 82.6 us -> 82.4 us (level)
  transfers between devices with their start and end apart: 5 -> 5, of which waited for: 4 -> 4; matrix products, arithmetic and copies ran while one was open for 0% -> 0% of each run, Pallas kernels for 1% -> 2%
where the time goes in v6:
time: 82.4 us; the launch traced here: 82.2 us
  blocking collectives  29.6 us (36%)
  starting transfers between devices  26.5 us (32%)
  waiting for transfers between devices  19.1 us (23%)
  Pallas kernels  6.17 us (7%)
  between operations  0.85 us (1%)
    all_to_all x1, blocking collectives, shards(): lax.all_to_all(sent.reshape(NX * SENT, 1, LANES), 'comp', split_axis=0, c...  29.6 us
    all_to_all x1, waiting for transfers between devices, shards(): lax.all_to_all(by_row.reshape(NCOMP, 1, LANES), 'comp', split_axis=0, con...  16.8 us
    all_to_all x1, starting transfers between devices, shards(): lax.all_to_all(by_row.reshape(NCOMP, 1, LANES), 'comp', split_axis=0, con...  16.3 us
    ppermute x1, starting transfers between devices, shards(): theirs = lax.ppermute(mine, 'tile', swap)  5.87 us
    ppermute x1, starting transfers between devices, shards(): two = lax.ppermute(two, ('comp', 'tile'), pairs)  3.19 us
    pallas_call x1, Pallas kernels, shards(): call(by_row_kernel, 'h', 'h', f32(NCOMP, LANES), [held[0], sems, pltpu.VM...  1.93 us
    pallas_call x1, Pallas kernels, shards(): call(last_kernel, 'vvvv', 'hv', (f32(LOCAL, NX, LANES), f32(NSTEP, CELLS...  1.68 us
  transfers between devices with their start and end apart: 5, of which 4 were waited for; matrix products, arithmetic and copies ran while one was open for 0% of the time, Pallas kernels for 2%

profile of v6, /device:TPU:1, one launch (start us, length us, event | category | flops | bytes accessed | tf_op | source)
XLA Modules:
  0.0 82.2 jit_solution(2205622240273930818)
XLA Ops:
  0.6 0.0 copy-start.4
  0.6 0.0 copy-start.3
  0.7 0.0 copy-start.1
  0.7 0.0 copy-start.9
  0.7 0.0 copy-start.8
  0.7 0.0 copy-start.7
  0.7 1.9 %shard_map.122 = f32[1152,128]{1,0:T(8,128)} custom-call(f32[9,128,128]{2,1,0:T(8,128)} %in_ref.1), custom_call_target="tpu_custom_call" | custom-call | tf_op jit(solution)/shard_map/pallas_call | solution.py:385
  2.7 16.3 %all-to-all-start = ((f32[1152,1,128]{2,1,0:T(1,128)}), f32[1152,1,128]{2,1,0:T(1,128)S(1)}, u32[]{:S(2)}, u32[]{:S(2)}) async-start(f32[1152,1,128]{2,1,0:T(1,128)} %bitcast.28), calls=%async_computation | async-start | bytes 1179648 | tf_op jit(solution)/shard_map/all_to_all | solution.py:388
  19.1 1.0 %shard_map.123 = (f32[13,32,128]{2,1,0:T(8,128)S(1)}, f32[2,36,128]{2,1,0:T(8,128)S(1)}, f32[8,128]{1,0:T(8,128)S(1)}, f32[2,128,128]{2,1,0:T(8,128)S(1)}, bf16[...) custom-call(f32[2,1152,128]{2,1,0:T(8,128)S(1)} %bitcast.15, f32[2,128]{1,0:T(2,128)S(1)} %bitcast.26, ...), custom_call_target="tpu_custom_call" | custom-call | tf_op jit(solution)/shard_map/pallas_call | solution.py:390
  20.1 16.8 %all-to-all-done = f32[1152,1,128]{2,1,0:T(1,128)S(1)} async-done(((f32[1152,1,128]{2,1,0:T(1,128)}), f32[1152,1,128]{2,1,0:T(1,128)S(1)}, u32[]{:S(2)}, u32[]{:S(2)}) %all-to-all-start) | async-done | bytes 589856 | tf_op jit(solution)/shard_map/all_to_all | solution.py:388
  37.0 0.4 shard_map.124
  37.4 1.1 %collective-permute-start.2 = (f32[576,128]{1,0:T(8,128)S(1)}, f32[576,128]{1,0:T(8,128)S(1)}, u32[]{:S(2)}, u32[]{:S(2)}) collective-permute-start(f32[576,128]{1,0:T(8,128)S(1)} %get-tuple-element.26), channel_id=1, source_target_pairs={{0,2},{2,0},{4,6},{6,4},{8,10},{10,8},{12,14},{14,12},{16,18},{18,... | collective-permute-start | bytes 884744 | tf_op jit(solution)/shard_map/ppermute | solution.py:424
  38.4 3.2 %collective-permute-start = (f32[576,128]{1,0:T(8,128)S(1)}, f32[576,128]{1,0:T(8,128)S(1)}, u32[]{:S(2)}, u32[]{:S(2)}) collective-permute-start(f32[576,128]{1,0:T(8,128)S(1)} %get-tuple-element.21), channel_id=1, source_target_pairs={{2,4},{3,5},{4,2},{5,3},{6,8},{7,9},{8,6},{9,7},{10,12},{11,13},{1... | collective-permute-start | bytes 884744 | tf_op jit(solution)/shard_map/ppermute | solution.py:425
  41.6 0.0 collective-permute-start.1
  41.6 1.2 %collective-permute-done.1.edge_ref = f32[32,128]{1,0:T(8,128)S(1)} collective-permute-done((f32[32,128]{1,0:T(8,128)S(1)}, f32[32,128]{1,0:T(8,128)S(1)}, u32[]{:S(2)}, u32[]{:S(2)}) %collective-permute-start.1) | collective-permute-done | bytes 16416 | tf_op jit(solution)/shard_map/ppermute | solution.py:426
  42.9 0.2 collective-permute-done.2.one_ref
  43.0 0.3 shard_map.125
  43.3 0.0 collective-permute-done.two_ref
  43.3 0.6 shard_map.126
  44.0 29.6 %all_to_all.10 = f32[1280,1,128]{2,1,0:T(1,128)S(1)} all-to-all(f32[1280,1,128]{2,1,0:T(1,128)S(1)} %bitcast.21), channel_id=1, replica_groups=mesh['comp'=128,'tile'=2] {'comp'}, dimensions={0} | all-to-all | bytes 1310720 | tf_op jit(solution)/shard_map/all_to_all | solution.py:437
  73.5 0.2 shard_map.127.mine_ref
  73.7 5.9 %collective-permute-start.3 = (f32[136,128]{1,0:T(8,128)S(1)}, f32[136,128]{1,0:T(8,128)S(1)}, u32[]{:S(2)}, u32[]{:S(2)}) collective-permute-start(f32[136,128]{1,0:T(8,128)S(1)} %shard_map.127.mine_ref), channel_id=1, source_target_pairs={{0,1},{1,0},{2,3},{3,2},{4,5},{5,4},{6,7},{7,6},{8,9},{9,8},{10,11... | collective-permute-start | bytes 208904 | tf_op jit(solution)/shard_map/ppermute | solution.py:440
  79.6 0.9 %collective-permute-done.3.edges_ref = f32[136,128]{1,0:T(8,128)S(1)} collective-permute-done((f32[136,128]{1,0:T(8,128)S(1)}, f32[136,128]{1,0:T(8,128)S(1)}, u32[]{:S(2)}, u32[]{:S(2)}) %collective-permute-start.3) | collective-permute-done | bytes 69664 | tf_op jit(solution)/shard_map/ppermute | solution.py:440
  80.5 1.7 %shard_map.128 = (f32[9,128,128]{2,1,0:T(8,128)}, f32[2,8]{1,0:T(2,128)}) custom-call(f32[1280,128]{1,0:T(8,128)S(1)} %bitcast.20, f32[136,128]{1,0:T(8,128)S(1)} %shard_map.127.mine_ref, f32[136,128]{1,0:T(8,128)S(1)} %collective-permute-done.3.edges_ref, f32[2,128,128]{2,1,0:T(8,128)S(1)} %get-tuple-element.29.face_ref), custom_call_target="tpu_custom_call" | custom-call | tf_op jit(solution)/shard_map/pallas_call | solution.py:441
  (14 shorter events, 0.0 us)
Async XLA Ops:
  0.6 18.4 %copy-start.4 = (f32[4,1,128]{2,1,0:T(1,128)S(1)}, f32[4,1,128]{2,1,0:T(1,128)}, u32[]{:S(2)}) copy-start(f32[4,1,128]{2,1,0:T(1,128)} %param.21) | copy-start | bytes 6148
  0.6 18.4 %copy-start.3 = (s32[4,1,128]{2,1,0:T(1,128)S(1)}, s32[4,1,128]{2,1,0:T(1,128)}, u32[]{:S(2)}) copy-start(s32[4,1,128]{2,1,0:T(1,128)} %param.20) | copy-start | bytes 6148
  0.7 18.4 %copy-start.1 = (s32[128,256]{1,0:T(8,128)S(1)}, s32[128,256]{1,0:T(8,128)}, u32[]{:S(2)}) copy-start(s32[128,256]{1,0:T(8,128)} %mask_ref.1) | copy-start | bytes 393220
  0.7 18.4 %copy-start.9 = (f32[32]{0:T(128)S(1)}, f32[32]{0:T(128)}, u32[]{:S(2)}) copy-start(f32[32]{0:T(128)} %dissip_ref.1) | copy-start | bytes 388
  0.7 18.4 %copy-start.8 = (f32[32]{0:T(128)S(1)}, f32[32]{0:T(128)}, u32[]{:S(2)}) copy-start(f32[32]{0:T(128)} %growth_ref.1) | copy-start | bytes 388
  0.7 18.4 %copy-start.7 = (f32[32]{0:T(128)S(1)}, f32[32]{0:T(128)}, u32[]{:S(2)}) copy-start(f32[32]{0:T(128)} %courant_ref.1) | copy-start | bytes 388
  0.7 18.4 %copy-start.2 = (f32[32,1,128]{2,1,0:T(1,128)S(1)}, f32[32,1,128]{2,1,0:T(1,128)}, u32[]{:S(2)}) copy-start(f32[32,1,128]{2,1,0:T(1,128)} %param.15) | copy-start | bytes 49156
  0.7 18.4 %copy-start.6 = (f32[2,1,128]{2,1,0:T(1,128)S(1)}, f32[2,1,128]{2,1,0:T(1,128)}, u32[]{:S(2)}) copy-start(f32[2,1,128]{2,1,0:T(1,128)} %param.14) | copy-start | bytes 3076
  0.7 18.4 %copy-start.5 = (f32[2,1,128]{2,1,0:T(1,128)S(1)}, f32[2,1,128]{2,1,0:T(1,128)}, u32[]{:S(2)}) copy-start(f32[2,1,128]{2,1,0:T(1,128)} %param.13) | copy-start | bytes 3076
  0.7 18.4 %copy-start = (f32[2,1152,1,128]{3,2,1,0:T(1,128)S(1)}, f32[2,1152,1,128]{3,2,1,0:T(1,128)}, u32[]{:S(2)}) copy-start(f32[2,1152,1,128]{3,2,1,0:T(1,128)} %param.12) | copy-start | bytes 3538948
  2.7 34.3 %all-to-all-start = ((f32[1152,1,128]{2,1,0:T(1,128)}), f32[1152,1,128]{2,1,0:T(1,128)S(1)}, u32[]{:S(2)}, u32[]{:S(2)}) async-start(f32[1152,1,128]{2,1,0:T(1,128)} %bitcast.28), calls=%async_computation | async-start | bytes 1179648 | tf_op jit(solution)/shard_map/all_to_all | solution.py:388
  37.4 5.7 %collective-permute-start.2 = (f32[576,128]{1,0:T(8,128)S(1)}, f32[576,128]{1,0:T(8,128)S(1)}, u32[]{:S(2)}, u32[]{:S(2)}) collective-permute-start(f32[576,128]{1,0:T(8,128)S(1)} %get-tuple-element.26), channel_id=1, source_target_pairs={{0,2},{2,0},{4,6},{6,4},{8,10},{10,8},{12,14},{14,12},{16,18},{18,... | collective-permute-start | bytes 884744 | tf_op jit(solution)/shard_map/ppermute | solution.py:424
  38.4 4.9 %collective-permute-start = (f32[576,128]{1,0:T(8,128)S(1)}, f32[576,128]{1,0:T(8,128)S(1)}, u32[]{:S(2)}, u32[]{:S(2)}) collective-permute-start(f32[576,128]{1,0:T(8,128)S(1)} %get-tuple-element.21), channel_id=1, source_target_pairs={{2,4},{3,5},{4,2},{5,3},{6,8},{7,9},{8,6},{9,7},{10,12},{11,13},{1... | collective-permute-start | bytes 884744 | tf_op jit(solution)/shard_map/ppermute | solution.py:425
  41.6 1.2 %collective-permute-start.1 = (f32[32,128]{1,0:T(8,128)S(1)}, f32[32,128]{1,0:T(8,128)S(1)}, u32[]{:S(2)}, u32[]{:S(2)}) collective-permute-start(f32[32,128]{1,0:T(8,128)S(1)} %get-tuple-element.22), channel_id=1, source_target_pairs={{0,1},{1,0},{2,3},{3,2},{4,5},{5,4},{6,7},{7,6},{8,9},{9,8},{10,11... | collective-permute-start | bytes 49160 | tf_op jit(solution)/shard_map/ppermute | solution.py:426
  73.7 6.8 %collective-permute-start.3 = (f32[136,128]{1,0:T(8,128)S(1)}, f32[136,128]{1,0:T(8,128)S(1)}, u32[]{:S(2)}, u32[]{:S(2)}) collective-permute-start(f32[136,128]{1,0:T(8,128)S(1)} %shard_map.127.mine_ref), channel_id=1, source_target_pairs={{0,1},{1,0},{2,3},{3,2},{4,5},{5,4},{6,7},{7,6},{8,9},{9,8},{10,11... | collective-permute-start | bytes 208904 | tf_op jit(solution)/shard_map/ppermute | solution.py:440

commit v7 on v6

--- a/solution.py
+++ b/solution.py
@@ -176,27 +176,24 @@
     shared, stress = source_sums(adjoint_of, spectrum_ref, coef_ref, spread_ref, vec_ref, step)
     stress_ref[...] = jnp.broadcast_to(stress, (8, LANES))
     lane = lane_iota(8)
-    edges = [jnp.zeros((8, LANES), jnp.float32) for _ in range(NFREQ // 8)]
-
-    def store(b, p, d, value):
-        moved_ref[pl.ds(p * NFREQ + 8 * b, 8), :] = value
-        column = value[:, :1] if SIN[d] >= 0 else value[:, LANES - 1 :]
-        edges[b] = jnp.where(lane == p, column, edges[b])
-
-    source_update(adjoint_of, store, coef_ref, spread_ref, shared, step)
-    for b in range(NFREQ // 8):
-        edge_ref[8 * b : 8 * b + 8] = edges[b]
+    half = NDIR // 2
     odd = lax.axis_index("comp") % 2
-
-    @pl.when(odd == 1)
-    def _():
-        one_ref[...] = moved_ref[:HALF]
-        two_ref[...] = moved_ref[HALF:]
-
-    @pl.when(odd == 0)
-    def _():
-        one_ref[...] = moved_ref[HALF:]
-        two_ref[...] = moved_ref[:HALF]
+    for parity in range(2):
+
+        @pl.when(odd == parity)
+        def _():
+            edges = [jnp.zeros((8, LANES), jnp.float32) for _ in range(NFREQ // 8)]
+
+            def store(b, p, d, value):
+                moved_ref[pl.ds(p * NFREQ + 8 * b, 8), :] = value
+                sent_ref = one_ref if (p < half) == (parity == 1) else two_ref
+                sent_ref[pl.ds(p % half * NFREQ + 8 * b, 8), :] = value
+                column = value[:, :1] if SIN[d] >= 0 else value[:, LANES - 1 :]
+                edges[b] = jnp.where(lane == p, column, edges[b])
+
+            source_update(adjoint_of, store, coef_ref, spread_ref, shared, step)
+            for b in range(NFREQ // 8):
+                edge_ref[8 * b : 8 * b + 8] = edges[b]
 
 
 def propagate_half(east, moved_ref, near_ref, edge_ref, spectrum_ref, coef_ref, spread_ref, half_ref, sums_ref):
@@ -250,7 +247,6 @@
 ):
     step = 0
     odd = lax.axis_index("comp") % 2
-    even = jnp.broadcast_to(odd, (8, LANES)) == 0
     for parity, east in ((0, False), (1, True)):
 
         @pl.when(odd == parity)
@@ -278,17 +274,19 @@
     )
     out_ref[pl.ds(LOCAL, NX, stride=SENT), :] = cells
 
-    def adjoint_of(b, p, d):
-        east = p < NDIR // 2
-        rows = pl.ds((p if east else p - NDIR // 2) * NFREQ + 8 * b, 8)
-        done, here = done_ref[rows, :], half_ref[rows, :]
-        return jnp.where(even, done, here) if east else jnp.where(even, here, done)
-
     def store(b, p, d, value):
         at = 8 * b * QUART * SENT + d // LOCAL * SENT + d % LOCAL
         out_ref[pl.ds(at, 8, stride=QUART * SENT), :] = value
 
-    source_update(adjoint_of, store, coef_ref, spread_ref, shared, step)
+    for parity in range(2):
+
+        @pl.when(odd == parity)
+        def _():
+            def adjoint_of(b, p, d):
+                ref = done_ref if (p < NDIR // 2) == (parity == 0) else half_ref
+                return ref[pl.ds(p % (NDIR // 2) * NFREQ + 8 * b, 8), :]
+
+            source_update(adjoint_of, store, coef_ref, spread_ref, shared, step)
 
 
 def edges_kernel(arrived_ref, out_ref):

time: 82.4 us -> 82.5 us (level)
  no operation moved by 1% of the time
where the time goes in v7:
time: 82.5 us; the launch traced here: 82.3 us
  blocking collectives  29.8 us (36%)
  starting transfers between devices  26.3 us (32%)
  waiting for transfers between devices  19.1 us (23%)
  Pallas kernels  6.19 us (8%)
  between operations  0.85 us (1%)
    all_to_all x1, blocking collectives, shards(): lax.all_to_all(sent.reshape(NX * SENT, 1, LANES), 'comp', split_axis=0, c...  29.8 us
    all_to_all x1, waiting for transfers between devices, shards(): lax.all_to_all(by_row.reshape(NCOMP, 1, LANES), 'comp', split_axis=0, con...  16.8 us
    all_to_all x1, starting transfers between devices, shards(): lax.all_to_all(by_row.reshape(NCOMP, 1, LANES), 'comp', split_axis=0, con...  16.3 us
    ppermute x1, starting transfers between devices, shards(): theirs = lax.ppermute(mine, 'tile', swap)  5.66 us
    ppermute x1, starting transfers between devices, shards(): two = lax.ppermute(two, ('comp', 'tile'), pairs)  3.19 us
    pallas_call x1, Pallas kernels, shards(): call(by_row_kernel, 'h', 'h', f32(NCOMP, LANES), [held[0], sems, pltpu.VM...  1.93 us
    pallas_call x1, Pallas kernels, shards(): call(last_kernel, 'vvvv', 'hv', (f32(LOCAL, NX, LANES), f32(NSTEP, CELLS...  1.68 us
  transfers between devices with their start and end apart: 5, of which 4 were waited for; matrix products, arithmetic and copies ran while one was open for 0% of the time, Pallas kernels for 2%

profile of v7, /device:TPU:1, one launch (start us, length us, event | category | flops | bytes accessed | tf_op | source)
XLA Modules:
  0.0 82.3 jit_solution(886683556101153877)
XLA Ops:
  0.6 0.0 copy-start.4
  0.6 0.0 copy-start.3
  0.7 0.0 copy-start.1
  0.7 0.0 copy-start.9
  0.7 0.0 copy-start.8
  0.7 0.0 copy-start.7
  0.7 1.9 %shard_map.122 = f32[1152,128]{1,0:T(8,128)} custom-call(f32[9,128,128]{2,1,0:T(8,128)} %in_ref.1), custom_call_target="tpu_custom_call" | custom-call | tf_op jit(solution)/shard_map/pallas_call | solution.py:383
  2.7 16.3 %all-to-all-start = ((f32[1152,1,128]{2,1,0:T(1,128)}), f32[1152,1,128]{2,1,0:T(1,128)S(1)}, u32[]{:S(2)}, u32[]{:S(2)}) async-start(f32[1152,1,128]{2,1,0:T(1,128)} %bitcast.28), calls=%async_computation | async-start | bytes 1179648 | tf_op jit(solution)/shard_map/all_to_all | solution.py:386
  19.1 1.0 %shard_map.123 = (f32[13,32,128]{2,1,0:T(8,128)S(1)}, f32[2,36,128]{2,1,0:T(8,128)S(1)}, f32[8,128]{1,0:T(8,128)S(1)}, f32[2,128,128]{2,1,0:T(8,128)S(1)}, bf16[...) custom-call(f32[2,1152,128]{2,1,0:T(8,128)S(1)} %bitcast.15, f32[2,128]{1,0:T(2,128)S(1)} %bitcast.26, ...), custom_call_target="tpu_custom_call" | custom-call | tf_op jit(solution)/shard_map/pallas_call | solution.py:388
  20.1 16.8 %all-to-all-done = f32[1152,1,128]{2,1,0:T(1,128)S(1)} async-done(((f32[1152,1,128]{2,1,0:T(1,128)}), f32[1152,1,128]{2,1,0:T(1,128)S(1)}, u32[]{:S(2)}, u32[]{:S(2)}) %all-to-all-start) | async-done | bytes 589856 | tf_op jit(solution)/shard_map/all_to_all | solution.py:386
  37.0 0.4 shard_map.124
  37.3 1.1 %collective-permute-start.2 = (f32[576,128]{1,0:T(8,128)S(1)}, f32[576,128]{1,0:T(8,128)S(1)}, u32[]{:S(2)}, u32[]{:S(2)}) collective-permute-start(f32[576,128]{1,0:T(8,128)S(1)} %get-tuple-element.26), channel_id=1, source_target_pairs={{0,2},{2,0},{4,6},{6,4},{8,10},{10,8},{12,14},{14,12},{16,18},{18,... | collective-permute-start | bytes 884744 | tf_op jit(solution)/shard_map/ppermute | solution.py:422
  38.5 3.2 %collective-permute-start = (f32[576,128]{1,0:T(8,128)S(1)}, f32[576,128]{1,0:T(8,128)S(1)}, u32[]{:S(2)}, u32[]{:S(2)}) collective-permute-start(f32[576,128]{1,0:T(8,128)S(1)} %get-tuple-element.21), channel_id=1, source_target_pairs={{2,4},{3,5},{4,2},{5,3},{6,8},{7,9},{8,6},{9,7},{10,12},{11,13},{1... | collective-permute-start | bytes 884744 | tf_op jit(solution)/shard_map/ppermute | solution.py:423
  41.6 0.0 collective-permute-start.1
  41.6 1.2 %collective-permute-done.1.edge_ref = f32[32,128]{1,0:T(8,128)S(1)} collective-permute-done((f32[32,128]{1,0:T(8,128)S(1)}, f32[32,128]{1,0:T(8,128)S(1)}, u32[]{:S(2)}, u32[]{:S(2)}) %collective-permute-start.1) | collective-permute-done | bytes 16416 | tf_op jit(solution)/shard_map/ppermute | solution.py:424
  42.9 0.1 collective-permute-done.2.one_ref
  43.0 0.3 shard_map.125
  43.3 0.0 collective-permute-done.two_ref
  43.3 0.7 shard_map.126
  44.0 29.8 %all_to_all.10 = f32[1280,1,128]{2,1,0:T(1,128)S(1)} all-to-all(f32[1280,1,128]{2,1,0:T(1,128)S(1)} %bitcast.21), channel_id=1, replica_groups=mesh['comp'=128,'tile'=2] {'comp'}, dimensions={0} | all-to-all | bytes 1310720 | tf_op jit(solution)/shard_map/all_to_all | solution.py:435
  73.8 0.2 shard_map.127.mine_ref
  74.0 5.7 %collective-permute-start.3 = (f32[136,128]{1,0:T(8,128)S(1)}, f32[136,128]{1,0:T(8,128)S(1)}, u32[]{:S(2)}, u32[]{:S(2)}) collective-permute-start(f32[136,128]{1,0:T(8,128)S(1)} %shard_map.127.mine_ref), channel_id=1, source_target_pairs={{0,1},{1,0},{2,3},{3,2},{4,5},{5,4},{6,7},{7,6},{8,9},{9,8},{10,11... | collective-permute-start | bytes 208904 | tf_op jit(solution)/shard_map/ppermute | solution.py:438
  79.7 0.9 %collective-permute-done.3.edges_ref = f32[136,128]{1,0:T(8,128)S(1)} collective-permute-done((f32[136,128]{1,0:T(8,128)S(1)}, f32[136,128]{1,0:T(8,128)S(1)}, u32[]{:S(2)}, u32[]{:S(2)}) %collective-permute-start.3) | collective-permute-done | bytes 69664 | tf_op jit(solution)/shard_map/ppermute | solution.py:438
  80.6 1.7 %shard_map.128 = (f32[9,128,128]{2,1,0:T(8,128)}, f32[2,8]{1,0:T(2,128)}) custom-call(f32[1280,128]{1,0:T(8,128)S(1)} %bitcast.20, f32[136,128]{1,0:T(8,128)S(1)} %shard_map.127.mine_ref, f32[136,128]{1,0:T(8,128)S(1)} %collective-permute-done.3.edges_ref, f32[2,128,128]{2,1,0:T(8,128)S(1)} %get-tuple-element.29.face_ref), custom_call_target="tpu_custom_call" | custom-call | tf_op jit(solution)/shard_map/pallas_call | solution.py:439
  (14 shorter events, 0.0 us)
Async XLA Ops:
  0.6 18.4 %copy-start.4 = (f32[4,1,128]{2,1,0:T(1,128)S(1)}, f32[4,1,128]{2,1,0:T(1,128)}, u32[]{:S(2)}) copy-start(f32[4,1,128]{2,1,0:T(1,128)} %param.21) | copy-start | bytes 6148
  0.6 18.4 %copy-start.3 = (s32[4,1,128]{2,1,0:T(1,128)S(1)}, s32[4,1,128]{2,1,0:T(1,128)}, u32[]{:S(2)}) copy-start(s32[4,1,128]{2,1,0:T(1,128)} %param.20) | copy-start | bytes 6148
  0.7 18.4 %copy-start.1 = (s32[128,256]{1,0:T(8,128)S(1)}, s32[128,256]{1,0:T(8,128)}, u32[]{:S(2)}) copy-start(s32[128,256]{1,0:T(8,128)} %mask_ref.1) | copy-start | bytes 393220
  0.7 18.4 %copy-start.9 = (f32[32]{0:T(128)S(1)}, f32[32]{0:T(128)}, u32[]{:S(2)}) copy-start(f32[32]{0:T(128)} %dissip_ref.1) | copy-start | bytes 388
  0.7 18.4 %copy-start.8 = (f32[32]{0:T(128)S(1)}, f32[32]{0:T(128)}, u32[]{:S(2)}) copy-start(f32[32]{0:T(128)} %growth_ref.1) | copy-start | bytes 388
  0.7 18.4 %copy-start.7 = (f32[32]{0:T(128)S(1)}, f32[32]{0:T(128)}, u32[]{:S(2)}) copy-start(f32[32]{0:T(128)} %courant_ref.1) | copy-start | bytes 388
  0.7 18.4 %copy-start.2 = (f32[32,1,128]{2,1,0:T(1,128)S(1)}, f32[32,1,128]{2,1,0:T(1,128)}, u32[]{:S(2)}) copy-start(f32[32,1,128]{2,1,0:T(1,128)} %param.15) | copy-start | bytes 49156
  0.7 18.4 %copy-start.6 = (f32[2,1,128]{2,1,0:T(1,128)S(1)}, f32[2,1,128]{2,1,0:T(1,128)}, u32[]{:S(2)}) copy-start(f32[2,1,128]{2,1,0:T(1,128)} %param.14) | copy-start | bytes 3076
  0.7 18.4 %copy-start.5 = (f32[2,1,128]{2,1,0:T(1,128)S(1)}, f32[2,1,128]{2,1,0:T(1,128)}, u32[]{:S(2)}) copy-start(f32[2,1,128]{2,1,0:T(1,128)} %param.13) | copy-start | bytes 3076
  0.7 18.4 %copy-start = (f32[2,1152,1,128]{3,2,1,0:T(1,128)S(1)}, f32[2,1152,1,128]{3,2,1,0:T(1,128)}, u32[]{:S(2)}) copy-start(f32[2,1152,1,128]{3,2,1,0:T(1,128)} %param.12) | copy-start | bytes 3538948
  2.7 34.3 %all-to-all-start = ((f32[1152,1,128]{2,1,0:T(1,128)}), f32[1152,1,128]{2,1,0:T(1,128)S(1)}, u32[]{:S(2)}, u32[]{:S(2)}) async-start(f32[1152,1,128]{2,1,0:T(1,128)} %bitcast.28), calls=%async_computation | async-start | bytes 1179648 | tf_op jit(solution)/shard_map/all_to_all | solution.py:386
  37.3 5.7 %collective-permute-start.2 = (f32[576,128]{1,0:T(8,128)S(1)}, f32[576,128]{1,0:T(8,128)S(1)}, u32[]{:S(2)}, u32[]{:S(2)}) collective-permute-start(f32[576,128]{1,0:T(8,128)S(1)} %get-tuple-element.26), channel_id=1, source_target_pairs={{0,2},{2,0},{4,6},{6,4},{8,10},{10,8},{12,14},{14,12},{16,18},{18,... | collective-permute-start | bytes 884744 | tf_op jit(solution)/shard_map/ppermute | solution.py:422
  38.5 4.8 %collective-permute-start = (f32[576,128]{1,0:T(8,128)S(1)}, f32[576,128]{1,0:T(8,128)S(1)}, u32[]{:S(2)}, u32[]{:S(2)}) collective-permute-start(f32[576,128]{1,0:T(8,128)S(1)} %get-tuple-element.21), channel_id=1, source_target_pairs={{2,4},{3,5},{4,2},{5,3},{6,8},{7,9},{8,6},{9,7},{10,12},{11,13},{1... | collective-permute-start | bytes 884744 | tf_op jit(solution)/shard_map/ppermute | solution.py:423
  41.6 1.2 %collective-permute-start.1 = (f32[32,128]{1,0:T(8,128)S(1)}, f32[32,128]{1,0:T(8,128)S(1)}, u32[]{:S(2)}, u32[]{:S(2)}) collective-permute-start(f32[32,128]{1,0:T(8,128)S(1)} %get-tuple-element.22), channel_id=1, source_target_pairs={{0,1},{1,0},{2,3},{3,2},{4,5},{5,4},{6,7},{7,6},{8,9},{9,8},{10,11... | collective-permute-start | bytes 49160 | tf_op jit(solution)/shard_map/ppermute | solution.py:424
  74.0 6.6 %collective-permute-start.3 = (f32[136,128]{1,0:T(8,128)S(1)}, f32[136,128]{1,0:T(8,128)S(1)}, u32[]{:S(2)}, u32[]{:S(2)}) collective-permute-start(f32[136,128]{1,0:T(8,128)S(1)} %shard_map.127.mine_ref), channel_id=1, source_target_pairs={{0,1},{1,0},{2,3},{3,2},{4,5},{5,4},{6,7},{7,6},{8,9},{9,8},{10,11... | collective-permute-start | bytes 208904 | tf_op jit(solution)/shard_map/ppermute | solution.py:438

commit v8 on v7

--- a/solution.py
+++ b/solution.py
@@ -247,6 +247,7 @@
 ):
     step = 0
     odd = lax.axis_index("comp") % 2
+    even = jnp.broadcast_to(odd, (8, LANES)) == 0
     for parity, east in ((0, False), (1, True)):
 
         @pl.when(odd == parity)
@@ -274,19 +275,17 @@
     )
     out_ref[pl.ds(LOCAL, NX, stride=SENT), :] = cells
 
+    def adjoint_of(b, p, d):
+        east = p < NDIR // 2
+        rows = pl.ds((p if east else p - NDIR // 2) * NFREQ + 8 * b, 8)
+        done, here = done_ref[rows, :], half_ref[rows, :]
+        return jnp.where(even, done, here) if east else jnp.where(even, here, done)
+
     def store(b, p, d, value):
         at = 8 * b * QUART * SENT + d // LOCAL * SENT + d % LOCAL
         out_ref[pl.ds(at, 8, stride=QUART * SENT), :] = value
 
-    for parity in range(2):
-
-        @pl.when(odd == parity)
-        def _():
-            def adjoint_of(b, p, d):
-                ref = done_ref if (p < NDIR // 2) == (parity == 0) else half_ref
-                return ref[pl.ds(p % (NDIR // 2) * NFREQ + 8 * b, 8), :]
-
-            source_update(adjoint_of, store, coef_ref, spread_ref, shared, step)
+    source_update(adjoint_of, store, coef_ref, spread_ref, shared, step)
 
 
 def edges_kernel(arrived_ref, out_ref):

time: 82.5 us -> 82.4 us (level)
  no operation moved by 1% of the time
where the time goes in v8:
time: 82.4 us; the launch traced here: 82.2 us
  blocking collectives  29.8 us (36%)
  starting transfers between devices  26.3 us (32%)
  waiting for transfers between devices  19.1 us (23%)
  Pallas kernels  6.14 us (7%)
  between operations  0.85 us (1%)
    all_to_all x1, blocking collectives, shards(): lax.all_to_all(sent.reshape(NX * SENT, 1, LANES), 'comp', split_axis=0, c...  29.8 us
    all_to_all x1, waiting for transfers between devices, shards(): lax.all_to_all(by_row.reshape(NCOMP, 1, LANES), 'comp', split_axis=0, con...  16.8 us
    all_to_all x1, starting transfers between devices, shards(): lax.all_to_all(by_row.reshape(NCOMP, 1, LANES), 'comp', split_axis=0, con...  16.3 us
    ppermute x1, starting transfers between devices, shards(): theirs = lax.ppermute(mine, 'tile', swap)  5.66 us
    ppermute x1, starting transfers between devices, shards(): two = lax.ppermute(two, ('comp', 'tile'), pairs)  3.19 us
    pallas_call x1, Pallas kernels, shards(): call(by_row_kernel, 'h', 'h', f32(NCOMP, LANES), [held[0], sems, pltpu.VM...  1.93 us
    pallas_call x1, Pallas kernels, shards(): call(last_kernel, 'vvvv', 'hv', (f32(LOCAL, NX, LANES), f32(NSTEP, CELLS...  1.68 us
  transfers between devices with their start and end apart: 5, of which 4 were waited for; matrix products, arithmetic and copies ran while one was open for 0% of the time, Pallas kernels for 2%

profile of v8, /device:TPU:1, one launch (start us, length us, event | category | flops | bytes accessed | tf_op | source)
XLA Modules:
  0.0 82.2 jit_solution(1909326416682777841)
XLA Ops:
  0.6 0.0 copy-start.4
  0.6 0.0 copy-start.3
  0.7 0.0 copy-start.1
  0.7 0.0 copy-start.9
  0.7 0.0 copy-start.8
  0.7 0.0 copy-start.7
  0.7 1.9 %shard_map.122 = f32[1152,128]{1,0:T(8,128)} custom-call(f32[9,128,128]{2,1,0:T(8,128)} %in_ref.1), custom_call_target="tpu_custom_call" | custom-call | tf_op jit(solution)/shard_map/pallas_call | solution.py:382
  2.7 16.3 %all-to-all-start = ((f32[1152,1,128]{2,1,0:T(1,128)}), f32[1152,1,128]{2,1,0:T(1,128)S(1)}, u32[]{:S(2)}, u32[]{:S(2)}) async-start(f32[1152,1,128]{2,1,0:T(1,128)} %bitcast.28), calls=%async_computation | async-start | bytes 1179648 | tf_op jit(solution)/shard_map/all_to_all | solution.py:385
  19.1 1.0 %shard_map.123 = (f32[13,32,128]{2,1,0:T(8,128)S(1)}, f32[2,36,128]{2,1,0:T(8,128)S(1)}, f32[8,128]{1,0:T(8,128)S(1)}, f32[2,128,128]{2,1,0:T(8,128)S(1)}, bf16[...) custom-call(f32[2,1152,128]{2,1,0:T(8,128)S(1)} %bitcast.15, f32[2,128]{1,0:T(2,128)S(1)} %bitcast.26, ...), custom_call_target="tpu_custom_call" | custom-call | tf_op jit(solution)/shard_map/pallas_call | solution.py:387
  20.1 16.8 %all-to-all-done = f32[1152,1,128]{2,1,0:T(1,128)S(1)} async-done(((f32[1152,1,128]{2,1,0:T(1,128)}), f32[1152,1,128]{2,1,0:T(1,128)S(1)}, u32[]{:S(2)}, u32[]{:S(2)}) %all-to-all-start) | async-done | bytes 589856 | tf_op jit(solution)/shard_map/all_to_all | solution.py:385
  37.0 0.4 shard_map.124
  37.3 1.1 %collective-permute-start.2 = (f32[576,128]{1,0:T(8,128)S(1)}, f32[576,128]{1,0:T(8,128)S(1)}, u32[]{:S(2)}, u32[]{:S(2)}) collective-permute-start(f32[576,128]{1,0:T(8,128)S(1)} %get-tuple-element.26), channel_id=1, source_target_pairs={{0,2},{2,0},{4,6},{6,4},{8,10},{10,8},{12,14},{14,12},{16,18},{18,... | collective-permute-start | bytes 884744 | tf_op jit(solution)/shard_map/ppermute | solution.py:421
  38.5 3.2 %collective-permute-start = (f32[576,128]{1,0:T(8,128)S(1)}, f32[576,128]{1,0:T(8,128)S(1)}, u32[]{:S(2)}, u32[]{:S(2)}) collective-permute-start(f32[576,128]{1,0:T(8,128)S(1)} %get-tuple-element.21), channel_id=1, source_target_pairs={{2,4},{3,5},{4,2},{5,3},{6,8},{7,9},{8,6},{9,7},{10,12},{11,13},{1... | collective-permute-start | bytes 884744 | tf_op jit(solution)/shard_map/ppermute | solution.py:422
  41.6 0.0 collective-permute-start.1
  41.6 1.2 %collective-permute-done.1.edge_ref = f32[32,128]{1,0:T(8,128)S(1)} collective-permute-done((f32[32,128]{1,0:T(8,128)S(1)}, f32[32,128]{1,0:T(8,128)S(1)}, u32[]{:S(2)}, u32[]{:S(2)}) %collective-permute-start.1) | collective-permute-done | bytes 16416 | tf_op jit(solution)/shard_map/ppermute | solution.py:423
  42.9 0.1 collective-permute-done.2.one_ref
  43.0 0.3 shard_map.125
  43.3 0.0 collective-permute-done.two_ref
  43.3 0.6 shard_map.126
  43.9 29.8 %all_to_all.10 = f32[1280,1,128]{2,1,0:T(1,128)S(1)} all-to-all(f32[1280,1,128]{2,1,0:T(1,128)S(1)} %bitcast.21), channel_id=1, replica_groups=mesh['comp'=128,'tile'=2] {'comp'}, dimensions={0} | all-to-all | bytes 1310720 | tf_op jit(solution)/shard_map/all_to_all | solution.py:434
  73.7 0.2 shard_map.127.mine_ref
  74.0 5.7 %collective-permute-start.3 = (f32[136,128]{1,0:T(8,128)S(1)}, f32[136,128]{1,0:T(8,128)S(1)}, u32[]{:S(2)}, u32[]{:S(2)}) collective-permute-start(f32[136,128]{1,0:T(8,128)S(1)} %shard_map.127.mine_ref), channel_id=1, source_target_pairs={{0,1},{1,0},{2,3},{3,2},{4,5},{5,4},{6,7},{7,6},{8,9},{9,8},{10,11... | collective-permute-start | bytes 208904 | tf_op jit(solution)/shard_map/ppermute | solution.py:437
  79.6 0.9 %collective-permute-done.3.edges_ref = f32[136,128]{1,0:T(8,128)S(1)} collective-permute-done((f32[136,128]{1,0:T(8,128)S(1)}, f32[136,128]{1,0:T(8,128)S(1)}, u32[]{:S(2)}, u32[]{:S(2)}) %collective-permute-start.3) | collective-permute-done | bytes 69664 | tf_op jit(solution)/shard_map/ppermute | solution.py:437
  80.5 1.7 %shard_map.128 = (f32[9,128,128]{2,1,0:T(8,128)}, f32[2,8]{1,0:T(2,128)}) custom-call(f32[1280,128]{1,0:T(8,128)S(1)} %bitcast.20, f32[136,128]{1,0:T(8,128)S(1)} %shard_map.127.mine_ref, f32[136,128]{1,0:T(8,128)S(1)} %collective-permute-done.3.edges_ref, f32[2,128,128]{2,1,0:T(8,128)S(1)} %get-tuple-element.29.face_ref), custom_call_target="tpu_custom_call" | custom-call | tf_op jit(solution)/shard_map/pallas_call | solution.py:438
  (14 shorter events, 0.0 us)
Async XLA Ops:
  0.6 18.4 %copy-start.4 = (f32[4,1,128]{2,1,0:T(1,128)S(1)}, f32[4,1,128]{2,1,0:T(1,128)}, u32[]{:S(2)}) copy-start(f32[4,1,128]{2,1,0:T(1,128)} %param.21) | copy-start | bytes 6148
  0.6 18.4 %copy-start.3 = (s32[4,1,128]{2,1,0:T(1,128)S(1)}, s32[4,1,128]{2,1,0:T(1,128)}, u32[]{:S(2)}) copy-start(s32[4,1,128]{2,1,0:T(1,128)} %param.20) | copy-start | bytes 6148
  0.7 18.4 %copy-start.1 = (s32[128,256]{1,0:T(8,128)S(1)}, s32[128,256]{1,0:T(8,128)}, u32[]{:S(2)}) copy-start(s32[128,256]{1,0:T(8,128)} %mask_ref.1) | copy-start | bytes 393220
  0.7 18.4 %copy-start.9 = (f32[32]{0:T(128)S(1)}, f32[32]{0:T(128)}, u32[]{:S(2)}) copy-start(f32[32]{0:T(128)} %dissip_ref.1) | copy-start | bytes 388
  0.7 18.4 %copy-start.8 = (f32[32]{0:T(128)S(1)}, f32[32]{0:T(128)}, u32[]{:S(2)}) copy-start(f32[32]{0:T(128)} %growth_ref.1) | copy-start | bytes 388
  0.7 18.4 %copy-start.7 = (f32[32]{0:T(128)S(1)}, f32[32]{0:T(128)}, u32[]{:S(2)}) copy-start(f32[32]{0:T(128)} %courant_ref.1) | copy-start | bytes 388
  0.7 18.4 %copy-start.2 = (f32[32,1,128]{2,1,0:T(1,128)S(1)}, f32[32,1,128]{2,1,0:T(1,128)}, u32[]{:S(2)}) copy-start(f32[32,1,128]{2,1,0:T(1,128)} %param.15) | copy-start | bytes 49156
  0.7 18.4 %copy-start.6 = (f32[2,1,128]{2,1,0:T(1,128)S(1)}, f32[2,1,128]{2,1,0:T(1,128)}, u32[]{:S(2)}) copy-start(f32[2,1,128]{2,1,0:T(1,128)} %param.14) | copy-start | bytes 3076
  0.7 18.4 %copy-start.5 = (f32[2,1,128]{2,1,0:T(1,128)S(1)}, f32[2,1,128]{2,1,0:T(1,128)}, u32[]{:S(2)}) copy-start(f32[2,1,128]{2,1,0:T(1,128)} %param.13) | copy-start | bytes 3076
  0.7 18.4 %copy-start = (f32[2,1152,1,128]{3,2,1,0:T(1,128)S(1)}, f32[2,1152,1,128]{3,2,1,0:T(1,128)}, u32[]{:S(2)}) copy-start(f32[2,1152,1,128]{3,2,1,0:T(1,128)} %param.12) | copy-start | bytes 3538948
  2.7 34.3 %all-to-all-start = ((f32[1152,1,128]{2,1,0:T(1,128)}), f32[1152,1,128]{2,1,0:T(1,128)S(1)}, u32[]{:S(2)}, u32[]{:S(2)}) async-start(f32[1152,1,128]{2,1,0:T(1,128)} %bitcast.28), calls=%async_computation | async-start | bytes 1179648 | tf_op jit(solution)/shard_map/all_to_all | solution.py:385
  37.3 5.7 %collective-permute-start.2 = (f32[576,128]{1,0:T(8,128)S(1)}, f32[576,128]{1,0:T(8,128)S(1)}, u32[]{:S(2)}, u32[]{:S(2)}) collective-permute-start(f32[576,128]{1,0:T(8,128)S(1)} %get-tuple-element.26), channel_id=1, source_target_pairs={{0,2},{2,0},{4,6},{6,4},{8,10},{10,8},{12,14},{14,12},{16,18},{18,... | collective-permute-start | bytes 884744 | tf_op jit(solution)/shard_map/ppermute | solution.py:421
  38.5 4.8 %collective-permute-start = (f32[576,128]{1,0:T(8,128)S(1)}, f32[576,128]{1,0:T(8,128)S(1)}, u32[]{:S(2)}, u32[]{:S(2)}) collective-permute-start(f32[576,128]{1,0:T(8,128)S(1)} %get-tuple-element.21), channel_id=1, source_target_pairs={{2,4},{3,5},{4,2},{5,3},{6,8},{7,9},{8,6},{9,7},{10,12},{11,13},{1... | collective-permute-start | bytes 884744 | tf_op jit(solution)/shard_map/ppermute | solution.py:422
  41.6 1.2 %collective-permute-start.1 = (f32[32,128]{1,0:T(8,128)S(1)}, f32[32,128]{1,0:T(8,128)S(1)}, u32[]{:S(2)}, u32[]{:S(2)}) collective-permute-start(f32[32,128]{1,0:T(8,128)S(1)} %get-tuple-element.22), channel_id=1, source_target_pairs={{0,1},{1,0},{2,3},{3,2},{4,5},{5,4},{6,7},{7,6},{8,9},{9,8},{10,11... | collective-permute-start | bytes 49160 | tf_op jit(solution)/shard_map/ppermute | solution.py:423
  74.0 6.6 %collective-permute-start.3 = (f32[136,128]{1,0:T(8,128)S(1)}, f32[136,128]{1,0:T(8,128)S(1)}, u32[]{:S(2)}, u32[]{:S(2)}) collective-permute-start(f32[136,128]{1,0:T(8,128)S(1)} %shard_map.127.mine_ref), channel_id=1, source_target_pairs={{0,1},{1,0},{2,3},{3,2},{4,5},{5,4},{6,7},{7,6},{8,9},{9,8},{10,11... | collective-permute-start | bytes 208904 | tf_op jit(solution)/shard_map/ppermute | solution.py:437
